TPU v7x, 512 devices: a whole 4x8x8 slice. The times are simulated.
512 devices in a mesh: section: 64 (over y_lo, z, x), tensor: 8 (over y_hi, core).
Axes of the slice: x: 4, y: 8 (y_hi: 4, y_lo: 2; y = y_hi * 2 + y_lo), z: 8, core: 2. Of those that a mesh axis runs over, the one named last changes fastest.
Arguments:
- outgoing: bfloat16 [16384, 512], P('section'), may hold values from -6 to 6
- returning: bfloat16 [16384, 512], P('section'), may hold values from -6 to 6
- token_ids: int32 [16384], P('section'), may hold values from 0 to 65535
- shared_basis: bfloat16 [512, 8192], P('section'), may hold values from -0.25 to 0.25
- embed_table: bfloat16 [8192, 65536], P(('tensor', 'section')), may hold values from -41 to 41
- norm_gain: float32 [64, 8192], P('section'), may hold values from 0.1 to 1.9
- value_weight: bfloat16 [64, 8192, 1024], P('section', None, 'tensor'), may hold values from -1 to 1
- write_basis: bfloat16 [64, 1024, 512], P('section', 'tensor'), may hold values from -2 to 2
- head_logits: bfloat16 [64, 8, 256, 256], P('section', 'tensor'), may hold values from -4 to 306, as said below
Outputs:
- next_outgoing: bfloat16 [16384, 512], P('section')
- next_returning: bfloat16 [16384, 512], P('section')
- grad_write_basis: float32 [64, 1024, 512], P('section', 'tensor')
- grad_norm_gain: bfloat16 [64, 8192], P('section')
Inputs may be any that keep to these rules, and one draw needn't show every extreme that they name: `head_logits`: entries above the diagonal are not read.
All inputs are finite; a program needn't handle non-finite values.
Results may differ from a plain program's by a relative error of at most 0.018.
Values may be sent and summed in bfloat16 or wider, within the bound.
A program may use at most 128 MiB of HBM per device.

v0:
```python
import jax
import jax.numpy as jnp
from jax import lax
from jax.sharding import PartitionSpec as P

D = 8192
HD = 128


def shifted(block, axis, distance):
    devices = range(lax.axis_size(axis))
    route = [(i - distance, i) for i in devices if i - distance in devices]
    return lax.ppermute(block, axis, route)


def causal_weights(head_logits):
    key_count = head_logits.shape[-1]
    causal = jnp.arange(key_count)[:, None] >= jnp.arange(key_count)[None, :]
    scores = jnp.where(causal[None], head_logits.astype(jnp.float32), -1e30)
    highest = jnp.max(scores, axis=-1, keepdims=True)
    weights = jnp.exp(scores - highest)
    return (weights / jnp.sum(weights, axis=-1, keepdims=True)).astype(jnp.bfloat16)


def shards(
    outgoing,
    returning,
    token_ids,
    shared_basis,
    embed_table,
    norm_gain,
    value_weight,
    write_basis,
    head_logits,
):
    section_count = lax.axis_size("section")
    section_index = lax.axis_index("section")
    tensor_index = lax.axis_index("tensor")
    tok_rows = outgoing.shape[0]
    from_before = shifted(outgoing, "section", 1)
    from_after = shifted(returning, "section", -1)
    cotangent = jnp.where(section_index == section_count - 1, returning, from_after)
    all_ids = lax.all_gather(token_ids, "section", axis=0, tiled=True)
    basis_whole = lax.all_gather(shared_basis, "section", axis=0, tiled=True)
    feature_rows = embed_table.shape[0]
    looked_up = jnp.take(embed_table, all_ids.reshape(section_count, tok_rows), axis=1)
    arrived = lax.all_to_all(looked_up, "section", split_axis=1, concat_axis=1, tiled=True)
    block_width = feature_rows * section_count
    embed_part = jnp.transpose(arrived, (2, 1, 0)).reshape(tok_rows, block_width)
    basis_cols = lax.dynamic_slice_in_dim(basis_whole, tensor_index * block_width, block_width, 1)
    rebuilt_part = jnp.dot(
        from_before, basis_cols, preferred_element_type=jnp.float32
    ) + embed_part.astype(jnp.float32)
    rebuilt = lax.all_gather(rebuilt_part.astype(jnp.bfloat16), "tensor", axis=1, tiled=True)
    residual = rebuilt.astype(jnp.float32)
    gain_row = norm_gain[0]
    spread = jnp.sqrt(jnp.mean(residual * residual, axis=-1, keepdims=True) + 1e-05)
    normed = (residual / spread * gain_row).astype(jnp.bfloat16)
    values = jnp.dot(normed, value_weight[0], preferred_element_type=jnp.float32).astype(
        jnp.bfloat16
    )
    local_heads = values.shape[1] // HD
    value_heads = values.reshape(tok_rows, local_heads, HD)
    head_weights = causal_weights(head_logits[0])
    attended = jnp.einsum(
        "hqk,khd->qhd", head_weights, value_heads, preferred_element_type=jnp.float32
    )
    attended = attended.astype(jnp.bfloat16).reshape(tok_rows, local_heads * HD)
    delta_part = jnp.dot(attended, write_basis[0], preferred_element_type=jnp.float32)
    grad_write = lax.dot_general(
        attended, cotangent, (((0,), (0,)), ((), ())), preferred_element_type=jnp.float32
    )
    grad_attended = lax.dot_general(
        cotangent, write_basis[0], (((1,), (1,)), ((), ())), preferred_element_type=jnp.float32
    )
    grad_attended = grad_attended.astype(jnp.bfloat16).reshape(tok_rows, local_heads, HD)
    grad_values = jnp.einsum(
        "hqk,qhd->khd", head_weights, grad_attended, preferred_element_type=jnp.float32
    )
    grad_values = grad_values.astype(jnp.bfloat16).reshape(tok_rows, local_heads * HD)
    grad_normed = lax.dot_general(
        grad_values, value_weight[0], (((1,), (1,)), ((), ())), preferred_element_type=jnp.float32
    )
    gain_part = jnp.sum(grad_normed * residual / spread, axis=0)
    inner_sum = jnp.sum(grad_normed * gain_row * residual, axis=-1, keepdims=True)
    grad_residual = gain_row * grad_normed / spread - residual * inner_sum / (D * spread**3)
    grad_upper = grad_residual.astype(jnp.bfloat16)
    grad_lower = (grad_residual - grad_upper.astype(jnp.float32)).astype(jnp.bfloat16)
    contract_rows = (((1,), (1,)), ((), ()))
    coefficient_part = lax.dot_general(
        grad_upper, basis_whole, contract_rows, preferred_element_type=jnp.float32
    )
    coefficient_part = coefficient_part + lax.dot_general(
        grad_lower, basis_whole, contract_rows, preferred_element_type=jnp.float32
    )
    delta_sum, coefficient_grad, gain_grad = (
        lax.psum(delta_part.astype(jnp.bfloat16), "tensor").astype(jnp.float32),
        lax.psum(coefficient_part.astype(jnp.bfloat16), "tensor").astype(jnp.float32),
        lax.psum(gain_part.astype(jnp.bfloat16), "tensor").astype(jnp.float32),
    )
    next_outgoing = (from_before.astype(jnp.float32) + delta_sum).astype(jnp.bfloat16)
    next_returning = (cotangent.astype(jnp.float32) + coefficient_grad).astype(jnp.bfloat16)
    grad_norm_gain = gain_grad.astype(jnp.bfloat16)
    return (next_outgoing, next_returning, grad_write[None], grad_norm_gain[None])


def solution(mesh):
    placed = (
        P("section", None),
        P("section", None),
        P("section"),
        P("section", None),
        P(("tensor", "section"), None),
        P("section", None),
        P("section", None, "tensor"),
        P("section", "tensor", None),
        P("section", "tensor", None, None),
    )
    return jax.shard_map(
        shards,
        mesh=mesh,
        in_specs=placed,
        out_specs=(
            P("section", None),
            P("section", None),
            P("section", "tensor", None),
            P("section", None),
        ),
        check_vma=False,
    )
```

profile of v0, /device:TPU:19, one launch (start us, length us, event | category | flops | bytes accessed | tf_op | source)
XLA Modules:
  0.0 511.4 jit_solution(15013797025379522703)
XLA Ops:
  7.2 0.0 copy-start
  7.2 0.0 all-gather.4.cloned.1.call-start
  7.2 0.7 all-gather.4.cloned.1.call-update
  7.9 0.0 copy-start.4
  7.9 12.4 %copy.17 = bf16[16,65536]{0,1:T(8,128)(2,1)} copy(bf16[16,65536]{1,0:T(8,128)(2,1)} %param.13) | data formatting | bytes 4194304 | tf_op args[4]
  20.3 0.0 copy-done.4
  20.3 134.5 %all-gather = s32[64,1,256]{2,1,0:T(1,128)S(1)} all-gather(s32[1,1,256]{2,1,0:T(1,128)S(1)} %bitcast.98), channel_id=1, replica_groups=mesh['section'=64,'tensor'=8] {'section'}, dimensions={0}, use_global_device_ids=true | all-gather | bytes 66560 | tf_op jit(solution)/shard_map/all_gather | solution.py:43
  154.8 0.1 compare_select_fusion
  154.9 0.0 copy-start.1
  154.9 63.4 %gather_fusion = bf16[16384,16]{1,0:T(8,128)(2,1)} fusion(bf16[16,65536]{0,1:T(8,128)(2,1)} %copy.17, s32[16384]{0:T(1024)S(1)} %broadcast_clamp_fusion), kind=kCustom, calls=%fused_computation | custom fusion | bytes 1114112 | tf_op jit(solution)/shard_map/jit(_take)/gather | solution.py:46
  218.4 3.5 copy.18
  221.9 0.9 select_bitcast_fusion
  222.7 10.0 %all-to-all-start = ((bf16[16,64,256]{2,0,1:T(8,128)(2,1)}), bf16[16,64,256]{2,0,1:T(8,128)(2,1)}, u32[]{:S(2)}, u32[]{:S(2)}) async-start(bf16[16,64,256]{2,0,1:T(8,128)(2,1)} %select_bitcast_fusion), calls=%async_computation | async-start | bytes 1048576 | tf_op jit(solution)/shard_map/all_to_all | solution.py:47
  232.8 0.0 all-gather.6.cloned.1.call-start
  232.8 3.1 collective-permute-start
  235.9 7.8 %all-to-all-done = bf16[16,64,256]{2,0,1:T(8,128)(2,1)} async-done(((bf16[16,64,256]{2,0,1:T(8,128)(2,1)}), bf16[16,64,256]{2,0,1:T(8,128)(2,1)}, u32[]{:S(2)}, u32[]{:S(2)}) %all-to-all-start) | async-done | bytes 524320 | tf_op jit(solution)/shard_map/all_to_all | solution.py:47
  243.8 1.2 convert_element_type.157
  245.0 0.3 collective-permute-done
  245.2 43.4 %all-gather.4.cloned.1.call-done = bf16[512,8192]{1,0:T(8,128)(2,1)} async-done(((bf16[8,8192]{1,0:T(8,128)(2,1)}), bf16[512,8192]{1,0:T(8,128)(2,1)}) %all-gather.4.cloned.1.call-update) | async-done | bytes 8388624 | tf_op jit(solution)/shard_map/all_gather | solution.py:44
  288.7 2.5 fusion.18
  291.2 0.0 all-gather.6.cloned.1.call-update
  291.2 0.0 all-reduce.3.cloned.1.call-start
  291.3 3.8 collective-permute-start.1
  295.1 1.0 fusion.39
  296.1 1.1 fusion.41
  297.2 2.5 collective-permute-done.1
  299.7 0.0 copy-done.1
  299.8 0.2 convolution_convert_fusion.1
  300.0 85.0 %all-gather.6.cloned.1.call-done = bf16[256,8192]{0,1:T(8,128)(2,1)} async-done(((bf16[256,1024]{0,1:T(8,128)(2,1)}), bf16[256,8192]{0,1:T(8,128)(2,1)}) %all-gather.6.cloned.1.call-update) | async-done | bytes 4194320 | tf_op jit(solution)/shard_map/all_gather | solution.py:54
  384.9 3.3 fusion
  388.3 0.0 copy-done
  388.3 0.0 copy-start.2
  388.3 0.0 copy-start.3
  388.3 4.9 fusion.26
  393.2 1.0 convolution_convert_fusion
  394.2 0.0 copy-done.2
  394.2 0.0 copy-done.3
  394.2 7.5 %fusion.7 = (bf16[8192]{0:T(1024)(128)(2,1)S(1)}, f32[256]{0:T(256)S(1)}, f32[256,8192]{0,1:T(8,128)}) fusion(bf16[256,8192]{0,1:T(8,128)(2,1)} %all-gather.6.cloned.1.call-done, f32[256]{0:T(256)S(1)} %get-tuple-element.9, f32[8192]{0:T(1024)S(1)} %bitcast.96, bf16[256,128]{1,0:T(8,128)(2,1)S(1)} %convolution_convert_fusion.1, ...), kind=kOutput, calls=%fused_computation.14 | convolution fusion | flops 568745728 | bytes 14929920 | tf_op jit(solution)/shard_map/dot_general | solution.py:81
  401.7 6.8 %fusion.5 = f32[256,8192]{0,1:T(8,128)S(1)} fusion(bf16[256,8192]{0,1:T(8,128)(2,1)} %all-gather.6.cloned.1.call-done, f32[256,8192]{0,1:T(8,128)} %get-tuple-element.10, f32[256]{0:T(256)S(1)} %get-tuple-element.8, f32[256]{0:T(256)S(1)} %get-tuple-element.5, f32[8192]{0:T(1024)S(1)} %bitcast.97, f32[256]{0:T(256)S(1)} %get-tuple-element.9), kind=kLoop, calls=%fused_computation.11 | loop fusion | flops 12582912 | bytes 21007360 | tf_op jit(solution)/shard_map/sub | solution.py:86
  408.5 6.0 %fusion.15 = f32[256,512]{1,0:T(8,128)S(1)} fusion(bf16[512,8192]{1,0:T(8,128)(2,1)} %all-gather.4.cloned.1.call-done, f32[256,8192]{0,1:T(8,128)S(1)} %fusion.5), kind=kOutput, calls=%fused_computation.21 | convolution fusion | flops 2149580800 | bytes 17301504 | tf_op jit(solution)/shard_map/dot_general | solution.py:90
  414.4 6.7 %fusion.20 = bf16[256,512]{1,0:T(8,128)(2,1)} fusion(f32[256,512]{1,0:T(8,128)S(1)} %fusion.15, bf16[512,8192]{1,0:T(8,128)(2,1)} %all-gather.4.cloned.1.call-done, f32[256,8192]{0,1:T(8,128)S(1)} %fusion.5), kind=kOutput, calls=%fused_computation.28 | convolution fusion | flops 2156134400 | bytes 17563648 | tf_op jit(solution)/shard_map/dot_general | solution.py:93
  421.1 0.0 all-reduce.3.cloned.1.call-update
  421.2 27.1 %psum.23 = bf16[1,8192]{1,0:T(2,128)(2,1)} all-reduce(bf16[1,8192]{1,0:T(2,128)(2,1)S(1)} %broadcast_in_dim.34), channel_id=1, replica_groups=mesh['section'=64,'tensor'=8] {'tensor'}, use_global_device_ids=true, to_apply=%region_7.8 | all-reduce | flops 8192 | bytes 32768 | tf_op jit(solution)/shard_map/psum | solution.py:99
  448.3 0.9 convolution_bitcast_fusion.1
  449.2 53.8 %all-reduce.3.cloned.1.call-done = (bf16[256,512]{1,0:T(8,128)(2,1)}, bf16[256,512]{1,0:T(8,128)(2,1)}) async-done(((bf16[256,512]{1,0:T(8,128)(2,1)}, bf16[256,512]{1,0:T(8,128)(2,1)}), (bf16[256,512]{1,0:T(8,128)(2,1)}, bf16[256,512]{1,0:T(8,128)(2,1)})) %all-reduce.3.cloned.1.call-update) | async-done | bytes 524304 | tf_op jit(solution)/shard_map/psum | solution.py:97
  502.9 1.9 add_convert_fusion
  (5 shorter events, 0.1 us)
Async XLA Ops:
  7.2 381.1 %copy-start = (bf16[1,8192,128]{2,1,0:T(8,128)(2,1)S(1)}, bf16[1,8192,128]{2,1,0:T(8,128)(2,1)}, u32[]{:S(2)}) copy-start(bf16[1,8192,128]{2,1,0:T(8,128)(2,1)} %param.15) | copy-start | bytes 6291460
  7.2 281.5 %all-gather.4.cloned.1.call-start = ((), (), s32[]{:S(2)}) async-start(), calls=%async_computation.1 | async-start | bytes 8519680 | tf_op jit(solution)/shard_map/all_gather | solution.py:44
  7.9 12.4 %copy-start.4 = (s32[256]{0:T(256)S(1)}, s32[256]{0:T(256)}, u32[]{:S(2)}) copy-start(s32[256]{0:T(256)} %param.11) | copy-start | bytes 3076
  154.9 144.8 %copy-start.1 = (bf16[1,128,512]{2,1,0:T(8,128)(2,1)S(1)}, bf16[1,128,512]{2,1,0:T(8,128)(2,1)}, u32[]{:S(2)}) copy-start(bf16[1,128,512]{2,1,0:T(8,128)(2,1)} %param.16) | copy-start | bytes 393220
  222.7 21.0 %all-to-all-start = ((bf16[16,64,256]{2,0,1:T(8,128)(2,1)}), bf16[16,64,256]{2,0,1:T(8,128)(2,1)}, u32[]{:S(2)}, u32[]{:S(2)}) async-start(bf16[16,64,256]{2,0,1:T(8,128)(2,1)} %select_bitcast_fusion), calls=%async_computation | async-start | bytes 1048576 | tf_op jit(solution)/shard_map/all_to_all | solution.py:47
  232.8 152.2 %all-gather.6.cloned.1.call-start = ((), (), s32[]{:S(2)}) async-start(), calls=%async_computation.2 | async-start | bytes 4718592 | tf_op jit(solution)/shard_map/all_gather | solution.py:54
  232.8 12.4 %collective-permute-start = (bf16[256,512]{1,0:T(8,128)(2,1)}, bf16[256,512]{1,0:T(8,128)(2,1)S(1)}, u32[]{:S(2)}, u32[]{:S(2)}) collective-permute-start(bf16[256,512]{1,0:T(8,128)(2,1)} %param.9), channel_id=1, source_target_pairs={{0,8},{8,16},{16,24},{24,32},{32,40},{40,48},{48,56},{56,64},{64,7... | collective-permute-start | bytes 786440 | tf_op jit(solution)/shard_map/ppermute | solution.py:13
  291.2 211.7 %all-reduce.3.cloned.1.call-start = ((), (), s32[]{:S(2)}) async-start(), calls=%async_computation.3 | async-start | bytes 1048576 | tf_op jit(solution)/shard_map/psum | solution.py:97
  291.3 8.5 %collective-permute-start.1 = (bf16[256,512]{1,0:T(8,128)(2,1)}, bf16[256,512]{1,0:T(8,128)(2,1)S(1)}, u32[]{:S(2)}, u32[]{:S(2)}) collective-permute-start(bf16[256,512]{1,0:T(8,128)(2,1)} %param.10), channel_id=1, source_target_pairs={{8,0},{16,8},{24,16},{32,24},{40,32},{48,40},{56,48},{64,56},{72,6... | collective-permute-start | bytes 786440 | tf_op jit(solution)/shard_map/ppermute | solution.py:13
  388.3 5.9 %copy-start.2 = (bf16[1,1,256,256]{3,2,1,0:T(8,128)(2,1)S(1)}, bf16[1,1,256,256]{3,2,1,0:T(8,128)(2,1)}, u32[]{:S(2)}) copy-start(bf16[1,1,256,256]{3,2,1,0:T(8,128)(2,1)} %param.17) | copy-start | bytes 393220
  388.3 5.9 %copy-start.3 = (f32[1,8192]{1,0:T(1,128)S(1)}, f32[1,8192]{1,0:T(1,128)}, u32[]{:S(2)}) copy-start(f32[1,8192]{1,0:T(1,128)} %param.14) | copy-start | bytes 98308
Sparse Core Ops, SparseCore 0:
  10.1 278.5 all-gather.3
  291.3 93.5 all-gather.5
  421.3 81.6 all-reduce.2
where the time goes:
time: 512 us; the launch traced here: 511 us
  waiting for transfers between devices  194 us (38%)
  blocking collectives  162 us (32%)
  local copies, waits for them, and re-layouts  79.3 us (15%)
  matrix products  29.7 us (6%)
  starting transfers between devices  17 us (3%)
  other arithmetic  16.3 us (3%)
  between operations  13.9 us (3%)
    all_gather x1, blocking collectives, shards(): all_ids = lax.all_gather(token_ids, 'section', axis=0, tiled=True)  135 us
    all_gather x1, waiting for transfers between devices, shards(): lax.all_gather(rebuilt_part.astype(jnp.bfloat16), 'tensor', axis=1, tiled...  85 us
    gather x2, local copies, waits for them, and re-layouts, shards(): jnp.take(embed_table, all_ids.reshape(section_count, tok_rows), axis=1)  66.9 us
    psum x1, waiting for transfers between devices, shards(): lax.psum(delta_part.astype(jnp.bfloat16), 'tensor').astype(jnp.float32)  53.8 us
    all_gather x1, waiting for transfers between devices, shards(): basis_whole = lax.all_gather(shared_basis, 'section', axis=0, tiled=True)  43.4 us
    psum x1, blocking collectives, shards(): lax.psum(gain_part.astype(jnp.bfloat16), 'tensor').astype(jnp.float32)  27.1 us
    unnamed x11, local copies, waits for them, and re-layouts  12.4 us
  transfers between devices with their start and end apart: 6, of which 6 were waited for; matrix products, arithmetic and copies ran while one was open for 17% of the time, Pallas kernels for 0%

commit v1 on v0

v1 whole, which is shorter than its diff:
```python
import functools

import jax
import jax.numpy as jnp
from jax import lax
from jax.experimental import pallas as pl
from jax.experimental.pallas import tpu as pltpu
from jax.sharding import PartitionSpec as P

D = 8192
HD = 128
R = 512
TOK = 256
VOCAB = 65536
FEAT = 16
NS = 64
NT = 8
WIDTH = FEAT * NS
ROWS = TOK // NT
MESH = pl.DeviceIdType.MESH
F32 = jnp.float32
BF16 = jnp.bfloat16


def dot(a, b):
    return jnp.dot(a, b, preferred_element_type=F32)


def dot_nt(a, b):
    return lax.dot_general(a, b, (((1,), (1,)), ((), ())), preferred_element_type=F32)


def wait_bytes(view, sem):
    pltpu.make_async_copy(view, view, sem).wait()


def kernel(
    outgoing, returning, ids, basis_own, table, gain, weight, write, logits,
    next_out, next_ret, grad_write, grad_gain,
    ids_own, ids_all, ids_scalar, coef, cot, piece, pieces, basis, w_all, table_t, stage,
    emb_out, emb_in, gv_own, gv_all, heads, gn, res_c, res, ng, sq_acc, in_acc,
    v_out, v_in, st_out, st_in, g_hi, g_lo, rs_out, rs_in, ag_own, ag_in, gg_own, gg_in,
    send, recv, local,
):
    s = lax.axis_index("section")
    t = lax.axis_index("tensor")

    def section_peer(k):
        return lax.rem(s + k, NS)

    def tensor_peer(k):
        return lax.rem(t + k, NT)

    own = ids[...]
    ids_own[0:2, :] = (own >> 10) * 128 + (own & 127)
    ids_own[2:4, :] = (own >> 7) & 7
    part = basis_own[:, pl.ds(pl.multiple_of(t * WIDTH, WIDTH), WIDTH)].astype(F32)
    piece[...] = jnp.concatenate([part[:, : WIDTH // 2], part[:, WIDTH // 2 :]], axis=0).astype(BF16)

    barrier = pltpu.get_barrier_semaphore()

    def greet_section(k, c):
        pl.semaphore_signal(barrier, inc=1, device_id=(section_peer(k), t), device_id_type=MESH)
        return c

    def greet_tensor(k, c):
        pl.semaphore_signal(barrier, inc=1, device_id=(s, tensor_peer(k)), device_id_type=MESH)
        return c

    lax.fori_loop(1, NS, greet_section, 0)
    lax.fori_loop(1, NT, greet_tensor, 0)
    pl.semaphore_wait(barrier, NS + NT - 2)

    def to_section(src, dst, which, p):
        pltpu.make_async_remote_copy(
            src_ref=src, dst_ref=dst, send_sem=send.at[which], recv_sem=recv.at[which],
            device_id=(p, t), device_id_type=MESH,
        ).start()

    def to_tensor(src, dst, which, p):
        pltpu.make_async_remote_copy(
            src_ref=src, dst_ref=dst, send_sem=send.at[which], recv_sem=recv.at[which],
            device_id=(s, p), device_id_type=MESH,
        ).start()

    def send_ids(k, c):
        to_section(ids_own, ids_all.at[s], 0, section_peer(k))
        return c

    lax.fori_loop(1, NS, send_ids, 0)
    ids_all[s] = ids_own[...]
    to_section(outgoing, coef, 1, section_peer(1))
    to_section(returning, cot, 2, section_peer(NS - 1))

    own_cols = pl.ds(pl.multiple_of(t * HD, HD), HD)

    def send_weight(k, c):
        p = tensor_peer(k)
        to_tensor(weight.at[0, pl.ds(pl.multiple_of(p * WIDTH, WIDTH), WIDTH)], w_all.at[:, own_cols], 4, p)
        return c

    lax.fori_loop(1, NT, send_weight, 0)
    w_here = pltpu.make_async_copy(
        weight.at[0, pl.ds(pl.multiple_of(t * WIDTH, WIDTH), WIDTH)], w_all.at[:, own_cols], local.at[0]
    )
    w_here.start()

    def send_basis(k, c):
        to_section(piece, pieces.at[s], 3, section_peer(k))
        return c

    lax.fori_loop(1, NS, send_basis, 0)
    pieces[s] = piece[...]

    def turn(b, c):
        x = table[:, pl.ds(pl.multiple_of(b * 1024, 1024), 1024)]
        x = jnp.concatenate([x[:, v * 128 : (v + 1) * 128] for v in range(8)], axis=0)
        table_t[pl.ds(pl.multiple_of(b * 128, 128), 128), :] = x.astype(F32).T
        return c

    lax.fori_loop(0, VOCAB // 1024, turn, 0)

    query = lax.broadcasted_iota(jnp.int32, (TOK, TOK), 0)
    key = lax.broadcasted_iota(jnp.int32, (TOK, TOK), 1)
    scores = jnp.where(query >= key, logits[0, 0].astype(F32), -1e30)
    expd = jnp.exp(scores - jnp.max(scores, axis=1, keepdims=True))
    soft = expd / jnp.sum(expd, axis=1, keepdims=True)
    heads[...] = soft.astype(BF16)
    to_turn = soft.T.astype(BF16)
    wait_bytes(cot, recv.at[2])

    @pl.when(s == NS - 1)
    def _():
        cot[...] = returning[...]

    ga = dot_nt(cot[...], write[0]).astype(BF16)
    gv_own[...] = dot(to_turn, ga).astype(BF16)

    def send_gv(k, c):
        to_tensor(gv_own, gv_all.at[:, own_cols], 5, tensor_peer(k))
        return c

    lax.fori_loop(1, NT, send_gv, 0)
    gv_all[:, own_cols] = gv_own[...]

    wait_bytes(ids_all.at[pl.ds(0, NS - 1)], recv.at[0])
    scalar_copy = pltpu.make_async_copy(ids_all, ids_scalar, local.at[1])
    scalar_copy.start()
    scalar_copy.wait()
    lane = lax.broadcasted_iota(jnp.int32, (8, 128), 1)
    sub = lax.broadcasted_iota(jnp.int32, (8, 128), 0)
    group = lane // FEAT

    def find(p, half):
        groups = jnp.broadcast_to(ids_all[p, pl.ds(2 + half, 1), :], (8, 128))
        for j in range(128):
            stage[pl.ds(j, 1), :] = table_t[pl.ds(ids_scalar[p, half, j], 1), :]
        outs = []
        for q in range(2):
            place = jnp.take_along_axis(groups, 16 * group + 8 * q + sub, axis=1) * FEAT + lane % FEAT
            acc = None
            for b in range(8):
                x = jnp.take_along_axis(stage[16 * b + 8 * q : 16 * b + 8 * q + 8, :], place, axis=1)
                acc = x if acc is None else jnp.where(group == b, x, acc)
            outs.append(acc)
        return jnp.concatenate(outs, axis=0).astype(BF16)

    def look_up(k, c):
        p = section_peer(k)

        def one_half(half, cc):
            emb_out[p, pl.ds(pl.multiple_of(half * 16, 16), 16), :] = find(p, half)
            return cc

        lax.fori_loop(0, 2, one_half, 0)

        to_section(emb_out.at[p], emb_in.at[s], 6, p)
        return c

    lax.fori_loop(1, NS, look_up, 0)

    def own_half(half, c):
        emb_in[s, pl.ds(pl.multiple_of(half * 16, 16), 16), :] = find(s, half)
        return c

    lax.fori_loop(0, 2, own_half, 0)

    wait_bytes(coef, recv.at[1])

    @pl.when(s == 0)
    def _():
        coef[...] = jnp.zeros_like(coef)

    wait_bytes(pieces.at[pl.ds(0, NS - 1)], recv.at[3])

    def order(i, c):
        x = pieces[pl.ds(i * 8, 8)].astype(F32)
        rows = pl.ds(pl.multiple_of(i * 64, 64), 64)
        for h in range(2):
            basis[rows, h * 512 : (h + 1) * 512] = x[:, 8 * h : 8 * h + 8, :].reshape(64, 512).astype(BF16)
        return c

    lax.fori_loop(0, NS // 8, order, 0)
    res_c[...] = dot(coef[...], basis[...])

    w_here.wait()
    wait_bytes(w_all.at[:, pl.ds(0, (NT - 1) * HD)], recv.at[4])
    wait_bytes(gv_all.at[:, pl.ds(0, (NT - 1) * HD)], recv.at[5])
    gn[...] = dot_nt(gv_all[...], w_all[...])

    wait_bytes(emb_in.at[pl.ds(0, NS - 1)], recv.at[6])
    sq_acc[...] = jnp.zeros_like(sq_acc)
    in_acc[...] = jnp.zeros_like(in_acc)
    lane16 = lax.broadcasted_iota(jnp.int32, (16, 128), 1) // FEAT

    def gain_row(u):
        return gain[:, pl.ds(pl.multiple_of(t * WIDTH + u * 128, 128), 128)]

    def assemble(u, c):
        cols = pl.ds(pl.multiple_of(u * 128, 128), 128)
        g_row = gain_row(u)
        for half in range(2):
            x = [emb_in[8 * u + v, 16 * half : 16 * half + 16, :].astype(F32) for v in range(8)]
            for d in (4, 2, 1):
                low = (lane16 & d) == 0
                y = list(x)
                for v in range(8):
                    if v & d == 0:
                        a, b = x[v], x[v + d]
                        y[v] = jnp.where(low, a, pltpu.roll(b, 16 * d, 1))
                        y[v + d] = jnp.where(low, pltpu.roll(a, 128 - 16 * d, 1), b)
                x = y
            for b in range(8):
                rows = slice(128 * half + 16 * b, 128 * half + 16 * b + 16)
                r = (res_c[rows, cols] + x[b]).astype(BF16)
                res[rows, cols] = r
                r = r.astype(F32)
                scaled = r * g_row
                ng[rows, cols] = scaled.astype(BF16)
                sq_acc[rows, :] += r * r
                in_acc[rows, :] += gn[rows, cols] * scaled
        return c

    lax.fori_loop(0, WIDTH // 128, assemble, 0)
    st_out[...] = jnp.zeros_like(st_out)
    st_out[0:1, :] = jnp.sum(sq_acc[...].T, axis=0, keepdims=True)
    st_out[1:2, :] = jnp.sum(in_acc[...].T, axis=0, keepdims=True)

    def send_stats(k, c):
        to_tensor(st_out, st_in.at[t], 8, tensor_peer(k))
        return c

    lax.fori_loop(1, NT, send_stats, 0)
    st_in[t] = st_out[...]
    for h in range(NT // 2):
        v = dot(ng[...], w_all[:, h * 256 : (h + 1) * 256]).astype(BF16)
        v_out[2 * h] = v[:, :HD]
        v_out[2 * h + 1] = v[:, HD:]

    def send_values(k, c):
        p = tensor_peer(k)
        to_tensor(v_out.at[p], v_in.at[t], 7, p)
        return c

    lax.fori_loop(1, NT, send_values, 0)
    v_in[t] = v_out[t]

    wait_bytes(st_in.at[pl.ds(0, NT - 1)], recv.at[8])
    total = st_in[0]
    for i in range(1, NT):
        total = total + st_in[i]
    spread = jnp.sqrt(total[0:1, :] / D + 1e-5)
    inv_row = 1.0 / spread
    back_row = total[1:2, :] * inv_row * inv_row * inv_row / D
    inv = jnp.broadcast_to(inv_row, (128, TOK)).T
    back = jnp.broadcast_to(back_row, (128, TOK)).T
    for u in range(WIDTH // 128):
        cols = slice(u * 128, (u + 1) * 128)
        n = gn[:, cols] * inv
        r = res[:, cols].astype(F32)
        gg_own[u : u + 1, :] = jnp.sum(n * r, axis=0, keepdims=True)
        g = n * gain_row(u) - r * back
        upper = g.astype(BF16)
        g_hi[:, cols] = upper
        g_lo[:, cols] = (g - upper.astype(F32)).astype(BF16)

    def send_gain(k, c):
        to_tensor(gg_own, gg_in.at[t], 11, tensor_peer(k))
        return c

    lax.fori_loop(1, NT, send_gain, 0)
    gg_in[t] = gg_own[...]
    grad = (dot_nt(g_hi[...], basis[...]) + dot_nt(g_lo[...], basis[...])).astype(BF16)
    for i in range(NT):
        rs_out[i, ROWS : 2 * ROWS, :] = grad[i * ROWS : (i + 1) * ROWS, :]

    wait_bytes(v_in.at[pl.ds(0, NT - 1)], recv.at[7])
    v = v_in[0].astype(F32)
    for i in range(1, NT):
        v = v + v_in[i].astype(F32)
    values = (v * inv).astype(BF16)
    attended = dot(heads[...], values)
    att = attended.astype(BF16)
    delta = dot(att, write[0]).astype(BF16)
    for i in range(NT):
        rs_out[i, 0:ROWS, :] = delta[i * ROWS : (i + 1) * ROWS, :]

    def send_rows(k, c):
        p = tensor_peer(k)
        to_tensor(rs_out.at[p], rs_in.at[t], 9, p)
        return c

    lax.fori_loop(1, NT, send_rows, 0)
    rs_in[t] = rs_out[t]
    grad_write[...] = dot(att.astype(F32).T.astype(BF16), cot[...])

    wait_bytes(rs_in.at[pl.ds(0, NT - 1)], recv.at[9])
    total = rs_in[0].astype(F32)
    for i in range(1, NT):
        total = total + rs_in[i].astype(F32)
    mine = pl.ds(pl.multiple_of(t * ROWS, ROWS), ROWS)
    ag_own[0:ROWS, :] = (coef[mine, :].astype(F32) + total[0:ROWS, :]).astype(BF16)
    ag_own[ROWS : 2 * ROWS, :] = (cot[mine, :].astype(F32) + total[ROWS : 2 * ROWS, :]).astype(BF16)

    def send_sums(k, c):
        to_tensor(ag_own, ag_in.at[t], 10, tensor_peer(k))
        return c

    lax.fori_loop(1, NT, send_sums, 0)
    ag_in[t] = ag_own[...]
    wait_bytes(gg_in.at[pl.ds(0, NT - 1)], recv.at[11])
    grad_gain[...] = jnp.concatenate(
        [gg_in[i, j : j + 1, :] for i in range(NT) for j in range(8)], axis=1
    ).astype(BF16)
    wait_bytes(ag_in.at[pl.ds(0, NT - 1)], recv.at[10])
    for i in range(NT):
        next_out[i * ROWS : (i + 1) * ROWS, :] = ag_in[i, 0:ROWS, :]
        next_ret[i * ROWS : (i + 1) * ROWS, :] = ag_in[i, ROWS : 2 * ROWS, :]

    wait_bytes(ids_all.at[pl.ds(0, NS - 1)], send.at[0])
    wait_bytes(coef, send.at[1])
    wait_bytes(cot, send.at[2])
    wait_bytes(pieces.at[pl.ds(0, NS - 1)], send.at[3])
    wait_bytes(w_all.at[:, pl.ds(0, (NT - 1) * HD)], send.at[4])
    wait_bytes(gv_all.at[:, pl.ds(0, (NT - 1) * HD)], send.at[5])
    wait_bytes(emb_in.at[pl.ds(0, NS - 1)], send.at[6])
    wait_bytes(v_in.at[pl.ds(0, NT - 1)], send.at[7])
    wait_bytes(st_in.at[pl.ds(0, NT - 1)], send.at[8])
    wait_bytes(rs_in.at[pl.ds(0, NT - 1)], send.at[9])
    wait_bytes(ag_in.at[pl.ds(0, NT - 1)], send.at[10])
    wait_bytes(gg_in.at[pl.ds(0, NT - 1)], send.at[11])


def shards(
    outgoing, returning, token_ids, shared_basis, embed_table, norm_gain, value_weight, write_basis, head_logits
):
    vmem = pl.BlockSpec(memory_space=pltpu.VMEM)
    hbm = pl.BlockSpec(memory_space=pl.ANY)
    next_out, next_ret, grad_write, grad_gain = pl.pallas_call(
        kernel,
        out_shape=(
            jax.ShapeDtypeStruct((TOK, R), BF16),
            jax.ShapeDtypeStruct((TOK, R), BF16),
            jax.ShapeDtypeStruct((HD, R), F32),
            jax.ShapeDtypeStruct((1, D), BF16),
        ),
        in_specs=[vmem, vmem, vmem, vmem, vmem, vmem, hbm, vmem, vmem],
        out_specs=(vmem, vmem, vmem, vmem),
        scratch_shapes=[
            pltpu.VMEM((4, 128), jnp.int32),
            pltpu.VMEM((NS, 4, 128), jnp.int32),
            pltpu.SMEM((NS, 4, 128), jnp.int32),
            pltpu.VMEM((TOK, R), BF16),
            pltpu.VMEM((TOK, R), BF16),
            pltpu.VMEM((16, WIDTH // 2), BF16),
            pltpu.VMEM((NS, 16, WIDTH // 2), BF16),
            pltpu.VMEM((R, WIDTH), BF16),
            pltpu.VMEM((WIDTH, NT * HD), BF16),
            pltpu.VMEM((VOCAB // 8, 128), F32),
            pltpu.VMEM((128, 128), F32),
            pltpu.VMEM((NS, 32, 128), BF16),
            pltpu.VMEM((NS, 32, 128), BF16),
            pltpu.VMEM((TOK, HD), BF16),
            pltpu.VMEM((TOK, NT * HD), BF16),
            pltpu.VMEM((TOK, TOK), BF16),
            pltpu.VMEM((TOK, WIDTH), F32),
            pltpu.VMEM((TOK, WIDTH), F32),
            pltpu.VMEM((TOK, WIDTH), BF16),
            pltpu.VMEM((TOK, WIDTH), BF16),
            pltpu.VMEM((TOK, 128), F32),
            pltpu.VMEM((TOK, 128), F32),
            pltpu.VMEM((NT, TOK, HD), BF16),
            pltpu.VMEM((NT, TOK, HD), BF16),
            pltpu.VMEM((8, TOK), F32),
            pltpu.VMEM((NT, 8, TOK), F32),
            pltpu.VMEM((TOK, WIDTH), BF16),
            pltpu.VMEM((TOK, WIDTH), BF16),
            pltpu.VMEM((NT, 2 * ROWS, R), BF16),
            pltpu.VMEM((NT, 2 * ROWS, R), BF16),
            pltpu.VMEM((2 * ROWS, R), BF16),
            pltpu.VMEM((NT, 2 * ROWS, R), BF16),
            pltpu.VMEM((8, 128), F32),
            pltpu.VMEM((NT, 8, 128), F32),
            pltpu.SemaphoreType.DMA((12,)),
            pltpu.SemaphoreType.DMA((12,)),
            pltpu.SemaphoreType.DMA((2,)),
        ],
        compiler_params=pltpu.CompilerParams(
            collective_id=0, has_side_effects=True, vmem_limit_bytes=52 * 2**20
        ),
        name="relay",
    )(
        outgoing, returning, token_ids.reshape(2, 128), shared_basis, embed_table, norm_gain, value_weight,
        write_basis, head_logits,
    )
    return (next_out, next_ret, grad_write[None], grad_gain)


def solution(mesh):
    placed = (
        P("section", None),
        P("section", None),
        P("section"),
        P("section", None),
        P(("tensor", "section"), None),
        P("section", None),
        P("section", None, "tensor"),
        P("section", "tensor", None),
        P("section", "tensor", None, None),
    )
    return jax.shard_map(
        shards,
        mesh=mesh,
        in_specs=placed,
        out_specs=(
            P("section", None),
            P("section", None),
            P("section", "tensor", None),
            P("section", None),
        ),
        check_vma=False,
    )
```

time: 512 us -> 160 us (0.31)
  the two profiles are of different devices: /device:TPU:19 before, /device:TPU:21 now
where the time goes in v1:
time: 160 us
  Pallas kernels  150 us (94%)
  local copies, waits for them, and re-layouts  8.76 us (5%)
    pallas_call x1, Pallas kernels, shards(): pl.pallas_call(kernel, out_shape=(jax.ShapeDtypeStruct((TOK, R), BF16), j...  150 us
    unnamed x18, local copies, waits for them, and re-layouts  8.76 us

profile of v1, /device:TPU:21, one launch (start us, length us, event | category | flops | bytes accessed | tf_op | source)
XLA Modules:
  0.0 159.8 jit_solution(16877740319056582940)
XLA Ops:
  0.6 0.0 copy-start
  0.6 0.9 copy-done
  1.6 0.0 copy-start.1
  1.6 0.9 copy-done.1
  2.5 0.0 copy-start.2
  2.5 0.9 copy-done.2
  3.4 0.0 copy-start.3
  3.4 0.9 copy-done.3
  4.3 0.0 copy-start.4
  4.3 0.9 copy-done.4
  5.2 0.0 copy-start.5
  5.3 0.8 copy-done.5
  6.0 0.0 copy-start.6
  6.0 0.7 copy-done.6
  6.7 150.4 %relay.1 = (bf16[256,512]{1,0:T(8,128)(2,1)S(1)}, bf16[256,512]{1,0:T(8,128)(2,1)S(1)}, f32[128,512]{1,0:T(8,128)S(1)}, bf16[1,8192]{1,0:T(2,128)(2,1)S(1)}) custom-call(bf16[256,512]{1,0:T(8,128)(2,1)S(1)} %copy-done, bf16[256,512]{1,0:T(8,128)(2,1)S(1)} %copy-done.1, s32[2,128]{1,0:T(2,128)S(1)} %bitcast.3, bf16[8,8192]{1,0:T(8,128)(2,1)S(1)} %copy-done.2, ...), custom_call_target="tpu_custom_call" | custom-call | tf_op jit(solution)/shard_map/relay/pallas_call | solution.py:359
  157.1 0.7 copy.17
  157.8 0.7 copy.18
  158.5 0.7 copy.19
  159.2 0.6 copy.20
Async XLA Ops:
  0.6 1.0 copy-start
  1.6 0.9 copy-start.1
  2.5 0.9 copy-start.2
  3.4 0.9 copy-start.3
  4.3 0.9 copy-start.4
  5.2 0.8 copy-start.5
  6.0 0.7 copy-start.6

commit v2 on v1

v2 whole, which is shorter than its diff:
```python
import functools

import jax
import jax.numpy as jnp
from jax import lax
from jax.experimental import pallas as pl
from jax.experimental.pallas import tpu as pltpu
from jax.sharding import PartitionSpec as P

D = 8192
HD = 128
R = 512
TOK = 256
VOCAB = 65536
FEAT = 16
NS = 64
NT = 8
WIDTH = FEAT * NS
ROWS = TOK // NT
HALF = TOK // 2
CHIPS = 4
CHIP_W = 2 * WIDTH
NX = 4
NZ = 8
AT_Z = 12
AT_X = 36
AT_ROWS = 44
AT_GRAD = 52
MESH = pl.DeviceIdType.MESH
F32 = jnp.float32
BF16 = jnp.bfloat16


def dot(a, b):
    return jnp.dot(a, b, preferred_element_type=F32)


def dot_nt(a, b):
    return lax.dot_general(a, b, (((1,), (1,)), ((), ())), preferred_element_type=F32)


def wait_bytes(view, sem):
    pltpu.make_async_copy(view, view, sem).wait()


def kernel(
    outgoing, returning, ids, basis_hbm, table_hbm, gain_hbm, weight, write_hbm, logits_hbm,
    next_out, next_ret, grad_write, grad_gain,
    basis_own, table, gain, write, logits,
    ids_raw, ids_own, ids_all, ids_scalar, coef, cot, pieces, basis, w_all, table_t, stage,
    emb_out, emb_in, gv_own, gv_all, heads, gn, gn_in, res_c, res, ng, acc, v_out, v_in, st_out, st_in,
    in_out, in_in, g_hi, g_lo, att_own, att_in, rs_out, rs_in, ag, ag_in, gg_own, gg_in,
    send, recv, local,
):
    s = lax.axis_index("section")
    t = lax.axis_index("tensor")
    chip = t // 2
    core = lax.rem(t, 2)
    other = 1 - core
    y_lo = s // (NX * NZ)
    z = lax.rem(s // NX, NZ)
    x = lax.rem(s, NX)

    def section_peer(k):
        return lax.rem(s + k, NS)

    def tensor_peer(k):
        return lax.rem(t + k, NT)

    def chip_peer(k):
        return lax.rem(chip + k, CHIPS)

    def fetch(src, dst, which):
        copy = pltpu.make_async_copy(src, dst, local.at[which])
        copy.start()
        return copy

    ids_copy = fetch(ids, ids_raw, 0)
    basis_copy = fetch(basis_hbm.at[:, pl.ds(pl.multiple_of(t * WIDTH, WIDTH), WIDTH)], basis_own, 1)
    table_copy = fetch(table_hbm, table, 2)
    logits_copy = fetch(logits_hbm.at[0, 0], logits, 3)
    write_copy = fetch(write_hbm.at[0], write.at[core], 4)
    gain_copy = fetch(gain_hbm.at[:, pl.ds(pl.multiple_of(chip * CHIP_W, CHIP_W), CHIP_W)], gain, 5)
    chip_rows = pl.ds(pl.multiple_of(chip * CHIP_W, CHIP_W), CHIP_W)
    own_cols = pl.ds(pl.multiple_of(chip * HD, HD), HD)
    w_copy = fetch(weight.at[0, chip_rows], w_all.at[:, own_cols], 6)

    barrier = pltpu.get_barrier_semaphore()

    def greet_section(k, c):
        pl.semaphore_signal(barrier, inc=1, device_id=(section_peer(k), t), device_id_type=MESH)
        return c

    def greet_tensor(k, c):
        pl.semaphore_signal(barrier, inc=1, device_id=(s, tensor_peer(k)), device_id_type=MESH)
        return c

    lax.fori_loop(1, NS, greet_section, 0)
    lax.fori_loop(1, NT, greet_tensor, 0)

    ids_copy.wait()
    own = ids_raw[...]
    ids_own[0:2, :] = (own >> 10) * 128 + (own & 127)
    ids_own[2:4, :] = (own >> 7) & 7
    basis_copy.wait()
    part = basis_own[...].astype(F32)
    pieces[x, z, y_lo] = jnp.concatenate([part[:, : WIDTH // 2], part[:, WIDTH // 2 :]], axis=0).astype(BF16)
    pl.semaphore_wait(barrier, NS + NT - 2)

    def push(src, dst, which, peer):
        pltpu.make_async_remote_copy(
            src_ref=src, dst_ref=dst, send_sem=send.at[which], recv_sem=recv.at[which],
            device_id=peer, device_id_type=MESH,
        ).start()

    def across(k):
        return (s, chip_peer(k) * 2 + core)

    partner = (s, chip * 2 + other)

    here = pl.ds(pl.multiple_of(core * HALF, HALF), HALF)
    there = pl.ds(pl.multiple_of(other * HALF, HALF), HALF)

    def send_ids(k, c):
        push(ids_own, ids_all.at[s], 0, (section_peer(k), t))
        return c

    lax.fori_loop(1, NS, send_ids, 0)
    ids_all[s] = ids_own[...]
    push(pieces.at[x, z, y_lo], pieces.at[x, z, y_lo], 3, (lax.rem(s + NS // 2, NS), t))
    write_copy.wait()
    push(write.at[core], write.at[core], 18, partner)

    @pl.when(s > 0)
    def _():
        push(returning.at[here], cot.at[here], 2, (section_peer(NS - 1), t))

    @pl.when(s < NS - 1)
    def _():
        push(outgoing.at[here], coef.at[here], 1, (section_peer(1), t))


    table_copy.wait()

    def turn(b, c):
        tile = table[:, pl.ds(pl.multiple_of(b * 1024, 1024), 1024)]
        tile = jnp.concatenate([tile[:, v * 128 : (v + 1) * 128] for v in range(8)], axis=0)
        table_t[pl.ds(pl.multiple_of(b * 128, 128), 128), :] = tile.astype(F32).T
        return c

    lax.fori_loop(0, VOCAB // 1024, turn, 0)
    for k in (2, 1, 3):
        rows = pl.ds(pl.multiple_of(chip_peer(k) * CHIP_W, CHIP_W), CHIP_W)
        push(weight.at[0, rows], w_all.at[:, own_cols], 4, across(k))

    wait_bytes(ids_all.at[pl.ds(0, NS - 1)], recv.at[0])
    scalar_copy = fetch(ids_all, ids_scalar, 0)
    scalar_copy.wait()
    lane = lax.broadcasted_iota(jnp.int32, (8, 128), 1)
    sub = lax.broadcasted_iota(jnp.int32, (8, 128), 0)
    group = lane // FEAT

    def find(p, half):
        groups = jnp.broadcast_to(ids_all[p, pl.ds(2 + half, 1), :], (8, 128))
        for j in range(128):
            stage[pl.ds(j, 1), :] = table_t[pl.ds(ids_scalar[p, half, j], 1), :]
        outs = []
        for q in range(2):
            place = jnp.take_along_axis(groups, 16 * group + 8 * q + sub, axis=1) * FEAT + lane % FEAT
            found = None
            for b in range(8):
                row = jnp.take_along_axis(stage[16 * b + 8 * q : 16 * b + 8 * q + 8, :], place, axis=1)
                found = row if found is None else jnp.where(group == b, row, found)
            outs.append(found)
        return jnp.concatenate(outs, axis=0).astype(BF16)

    def values_gradient():
        logits_copy.wait()
        query = lax.broadcasted_iota(jnp.int32, (TOK, TOK), 0)
        key = lax.broadcasted_iota(jnp.int32, (TOK, TOK), 1)
        scores = jnp.where(query >= key, logits[...].astype(F32), -1e30)
        expd = jnp.exp(scores - jnp.max(scores, axis=1, keepdims=True))
        soft = expd / jnp.sum(expd, axis=1, keepdims=True)
        heads[...] = soft.astype(BF16)
        to_turn = soft.T.astype(BF16)

        @pl.when(s < NS - 1)
        def _():
            wait_bytes(cot.at[here], recv.at[27])

        @pl.when(s == NS - 1)
        def _():
            last = pltpu.make_async_copy(returning, cot, local.at[0])
            last.start()
            last.wait()

        ga = dot_nt(cot[...], write[core]).astype(BF16)
        gv_own[...] = dot(to_turn, ga).astype(BF16)
        for j in (2, 1, 3):
            push(gv_own, gv_all.at[:, own_cols], 5, across(j))
        gv_all[:, own_cols] = gv_own[...]

    def look_up(k, c):
        p = section_peer(k)

        def one_half(half, cc):
            emb_out[p, pl.ds(pl.multiple_of(half * 16, 16), 16), :] = find(p, half)
            return cc

        lax.fori_loop(0, 2, one_half, 0)
        push(emb_out.at[p], emb_in.at[s], 6, (p, t))

        @pl.when(k == AT_Z)
        def _():
            wait_bytes(pieces.at[0, 0, 0], recv.at[3])

            def send_z(j, cc):
                push(pieces.at[x, z], pieces.at[x, z], 11, (y_lo * NX * NZ + lax.rem(z + j, NZ) * NX + x, t))
                return cc

            lax.fori_loop(1, NZ, send_z, 0)

        @pl.when(k == AT_X)
        def _():
            wait_bytes(pieces.at[0, pl.ds(0, NZ - 1)], recv.at[11])
            for j in (2, 1, 3):
                push(pieces.at[x], pieces.at[x], 12, (y_lo * NX * NZ + z * NX + lax.rem(x + j, NX), t))

        @pl.when(jnp.logical_and(k == AT_ROWS, s < NS - 1))
        def _():
            wait_bytes(cot.at[here], recv.at[2])
            push(cot.at[here], cot.at[here], 27, partner)

        @pl.when(jnp.logical_and(k == AT_ROWS, s > 0))
        def _():
            wait_bytes(coef.at[here], recv.at[1])
            push(coef.at[here], coef.at[here], 26, partner)

        @pl.when(k == AT_GRAD)
        def _():
            values_gradient()

        return c

    lax.fori_loop(1, NS, look_up, 0)

    def own_half(half, c):
        emb_in[s, pl.ds(pl.multiple_of(half * 16, 16), 16), :] = find(s, half)
        return c

    lax.fori_loop(0, 2, own_half, 0)

    wait_bytes(pieces.at[pl.ds(0, NX - 1)], recv.at[12])
    for lo in range(2):
        for zz in range(NZ):
            tile = pieces[:, zz, lo].astype(F32)
            for xx in range(NX):
                rows = slice((lo * NZ * NX + zz * NX + xx) * 8, (lo * NZ * NX + zz * NX + xx) * 8 + 8)
                if xx % 2 == 0:
                    pair = slice(rows.start, rows.start + 16)
                    for h in range(2):
                        both = jnp.concatenate([tile[xx, 8 * h : 8 * h + 8], tile[xx + 1, 8 * h : 8 * h + 8]], axis=0)
                        basis[core, pair, h * 512 : (h + 1) * 512] = both.astype(BF16)
    push(basis.at[core], basis.at[core], 13, partner)

    @pl.when(s > 0)
    def _():
        wait_bytes(coef.at[here], recv.at[26])

    @pl.when(s == 0)
    def _():
        coef[...] = jnp.zeros_like(coef)

    res_c[...] = dot(coef[...], basis[core])

    wait_bytes(emb_in.at[pl.ds(0, NS - 1)], recv.at[6])
    acc[...] = jnp.zeros_like(acc)
    lane16 = lax.broadcasted_iota(jnp.int32, (16, 128), 1) // FEAT

    def assemble(u, c):
        cols = pl.ds(pl.multiple_of(u * 128, 128), 128)
        for half in range(2):
            xs = [emb_in[8 * u + v, 16 * half : 16 * half + 16, :].astype(F32) for v in range(8)]
            for d in (4, 2, 1):
                low = (lane16 & d) == 0
                ys = list(xs)
                for v in range(8):
                    if v & d == 0:
                        a, b = xs[v], xs[v + d]
                        ys[v] = jnp.where(low, a, pltpu.roll(b, 16 * d, 1))
                        ys[v + d] = jnp.where(low, pltpu.roll(a, 128 - 16 * d, 1), b)
                xs = ys
            for b in range(8):
                rows = slice(128 * half + 16 * b, 128 * half + 16 * b + 16)
                r = (res_c[rows, cols] + xs[b]).astype(BF16)
                res[core, rows, cols] = r
                r = r.astype(F32)
                acc[rows, :] += r * r
        return c

    lax.fori_loop(0, WIDTH // 128, assemble, 0)
    push(res.at[core], res.at[core], 14, partner)
    st_out[...] = jnp.zeros_like(st_out)
    st_out[0:1, :] = jnp.sum(acc[...].T, axis=0, keepdims=True)

    def send_squares(k, c):
        push(st_out, st_in.at[t], 8, (s, tensor_peer(k)))
        return c

    lax.fori_loop(1, NT, send_squares, 0)
    st_in[t] = st_out[...]
    wait_bytes(st_in.at[pl.ds(0, NT - 1)], recv.at[8])
    total = st_in[0]
    for i in range(1, NT):
        total = total + st_in[i]
    inv_row = 1.0 / jnp.sqrt(total[0:1, :] / D + 1e-5)
    acc[...] = jnp.broadcast_to(inv_row, (128, TOK)).T
    gain_copy.wait()
    wait_bytes(res.at[0], recv.at[14])
    for i in range(2):

        def normalise(u, c):
            cols = pl.ds(pl.multiple_of(u * 128, 128), 128)
            wide = pl.ds(pl.multiple_of(i * WIDTH + u * 128, 128), 128)
            ng[:, wide] = (res[i, :, cols].astype(F32) * acc[...] * gain[:, wide]).astype(BF16)
            return c

        lax.fori_loop(0, WIDTH // 128, normalise, 0)

    w_copy.wait()
    wait_bytes(w_all.at[:, pl.ds(0, (CHIPS - 1) * HD)], recv.at[4])
    for h in range(2):
        v = dot(ng[...], w_all[:, h * 256 : (h + 1) * 256]).astype(BF16)
        v_out[2 * h] = v[:, :HD]
        v_out[2 * h + 1] = v[:, HD:]
    for k in (2, 1, 3):
        push(v_out.at[chip_peer(k)], v_in.at[chip], 7, across(k))
    v_in[chip] = v_out[chip]

    wait_bytes(gv_all.at[:, pl.ds(0, (CHIPS - 1) * HD)], recv.at[5])
    gn[...] = dot_nt(gv_all[...], w_all[...])
    push(gn.at[there], gn_in, 15, partner)
    wait_bytes(gn_in, recv.at[15])
    inv = acc[here, :]
    inner = jnp.zeros((HALF, 128), F32)
    for u in range(CHIP_W // 128):
        cols = slice(u * 128, (u + 1) * 128)
        narrow = slice(u % 8 * 128, (u % 8 + 1) * 128)
        n = gn[here, cols] + gn_in[:, cols]
        gn_in[:, cols] = n
        r = res[u // 8, here, narrow].astype(F32)
        inner = inner + n * gain[:, cols] * r
        gg_own[u : u + 1, :] = jnp.sum(n * inv * r, axis=0, keepdims=True)
    in_out[...] = jnp.broadcast_to(jnp.sum(inner.T, axis=0, keepdims=True), (8, HALF))
    for k in (2, 1, 3):
        push(in_out, in_in.at[chip], 16, across(k))
    in_in[chip] = in_out[...]
    wait_bytes(in_in.at[pl.ds(0, CHIPS - 1)], recv.at[16])
    total = in_in[0]
    for i in range(1, CHIPS):
        total = total + in_in[i]
    back = jnp.broadcast_to(total[0:1, :], (HALF, HALF)).T * inv * inv * inv / D
    for u in range(CHIP_W // 128):
        cols = slice(u * 128, (u + 1) * 128)
        narrow = slice(u % 8 * 128, (u % 8 + 1) * 128)
        g = gn_in[:, cols] * inv * gain[:, cols] - res[u // 8, here, narrow].astype(F32) * back
        upper = g.astype(BF16)
        g_hi[u // 8, :, narrow] = upper
        g_lo[u // 8, :, narrow] = (g - upper.astype(F32)).astype(BF16)
    wait_bytes(basis.at[0], recv.at[13])
    grad = dot_nt(g_hi[0], basis[0]) + dot_nt(g_lo[0], basis[0])
    grad = grad + (dot_nt(g_hi[1], basis[1]) + dot_nt(g_lo[1], basis[1]))
    grad = grad.astype(BF16)
    for i in range(CHIPS):
        rs_out[i, ROWS : 2 * ROWS, :] = grad[i * ROWS : (i + 1) * ROWS, :]

    wait_bytes(v_in.at[pl.ds(0, CHIPS - 1)], recv.at[7])
    v = v_in[0].astype(F32)
    for i in range(1, CHIPS):
        v = v + v_in[i].astype(F32)
    attended = dot(heads[...], v.astype(BF16))
    att_own[...] = attended.astype(BF16)
    push(att_own.at[there], att_in, 17, partner)
    wait_bytes(write.at[0], recv.at[18])
    delta = dot(att_own[here, :], write[core])
    wait_bytes(att_in, recv.at[17])
    delta = (delta + dot(att_in[...], write[other])).astype(BF16)
    for i in range(CHIPS):
        rs_out[i, 0:ROWS, :] = delta[i * ROWS : (i + 1) * ROWS, :]
    for k in (2, 1, 3):
        push(rs_out.at[chip_peer(k)], rs_in.at[chip], 9, across(k))
    rs_in[chip] = rs_out[chip]

    def send_gain(k, c):
        push(gg_own, gg_in.at[t], 10, (s, tensor_peer(k)))
        return c

    lax.fori_loop(1, NT, send_gain, 0)
    gg_in[t] = gg_own[...]
    grad_write[...] = dot(attended.T.astype(BF16), cot[...])

    wait_bytes(rs_in.at[pl.ds(0, CHIPS - 1)], recv.at[9])
    total = rs_in[0].astype(F32)
    for i in range(1, CHIPS):
        total = total + rs_in[i].astype(F32)
    mine = pl.ds(pl.multiple_of(core * HALF + chip * ROWS, ROWS), ROWS)
    ag[chip, 0:ROWS, :] = (coef[mine, :].astype(F32) + total[0:ROWS, :]).astype(BF16)
    ag[chip, ROWS : 2 * ROWS, :] = (cot[mine, :].astype(F32) + total[ROWS : 2 * ROWS, :]).astype(BF16)
    for k in (2, 1, 3):
        push(ag.at[chip], ag.at[chip], 19 + k, across(k))
    push(ag.at[chip], ag_in.at[chip], 19, partner)
    wait_bytes(gg_in.at[pl.ds(0, NT - 1)], recv.at[10])
    grad_gain[...] = jnp.concatenate(
        [gg_in[2 * i, j : j + 1, :] + gg_in[2 * i + 1, j : j + 1, :] for i in range(CHIPS) for j in range(16)], axis=1
    ).astype(BF16)
    for k in (1, 3, 2):
        wait_bytes(ag.at[0], recv.at[19 + k])
        come = chip_peer(CHIPS - k)
        push(ag.at[come], ag_in.at[come], 22 + k, partner)
    for i in range(CHIPS):
        rows = pl.ds(pl.multiple_of(core * HALF + i * ROWS, ROWS), ROWS)
        next_out[rows, :] = ag[i, 0:ROWS, :]
        next_ret[rows, :] = ag[i, ROWS : 2 * ROWS, :]
    for which in (19, 23, 24, 25):
        wait_bytes(ag_in.at[0], recv.at[which])
    for i in range(CHIPS):
        rows = pl.ds(pl.multiple_of(other * HALF + i * ROWS, ROWS), ROWS)
        next_out[rows, :] = ag_in[i, 0:ROWS, :]
        next_ret[rows, :] = ag_in[i, ROWS : 2 * ROWS, :]

    wait_bytes(ids_all.at[pl.ds(0, NS - 1)], send.at[0])

    @pl.when(s < NS - 1)
    def _():
        wait_bytes(coef.at[here], send.at[1])
        wait_bytes(cot.at[here], send.at[27])

    @pl.when(s > 0)
    def _():
        wait_bytes(cot.at[here], send.at[2])
        wait_bytes(coef.at[here], send.at[26])

    wait_bytes(pieces.at[0, 0, 0], send.at[3])
    wait_bytes(w_all.at[:, pl.ds(0, (CHIPS - 1) * HD)], send.at[4])
    wait_bytes(gv_all.at[:, pl.ds(0, (CHIPS - 1) * HD)], send.at[5])
    wait_bytes(emb_in.at[pl.ds(0, NS - 1)], send.at[6])
    wait_bytes(v_in.at[pl.ds(0, CHIPS - 1)], send.at[7])
    wait_bytes(st_in.at[pl.ds(0, NT - 1)], send.at[8])
    wait_bytes(rs_in.at[pl.ds(0, CHIPS - 1)], send.at[9])
    wait_bytes(gg_in.at[pl.ds(0, NT - 1)], send.at[10])
    wait_bytes(pieces.at[0, pl.ds(0, NZ - 1)], send.at[11])
    wait_bytes(pieces.at[pl.ds(0, NX - 1)], send.at[12])
    wait_bytes(basis.at[0], send.at[13])
    wait_bytes(res.at[0], send.at[14])
    wait_bytes(gn_in, send.at[15])
    wait_bytes(in_in.at[pl.ds(0, CHIPS - 1)], send.at[16])
    wait_bytes(att_in, send.at[17])
    wait_bytes(write.at[0], send.at[18])
    for which in (19, 20, 21, 22, 23, 24, 25):
        wait_bytes(ag_in.at[0], send.at[which])


def shards(
    outgoing, returning, token_ids, shared_basis, embed_table, norm_gain, value_weight, write_basis, head_logits
):
    vmem = pl.BlockSpec(memory_space=pltpu.VMEM)
    hbm = pl.BlockSpec(memory_space=pl.ANY)
    next_out, next_ret, grad_write, grad_gain = pl.pallas_call(
        kernel,
        out_shape=(
            jax.ShapeDtypeStruct((TOK, R), BF16),
            jax.ShapeDtypeStruct((TOK, R), BF16),
            jax.ShapeDtypeStruct((HD, R), F32),
            jax.ShapeDtypeStruct((1, D), BF16),
        ),
        in_specs=[hbm] * 9,
        out_specs=(vmem, vmem, vmem, vmem),
        scratch_shapes=[
            pltpu.VMEM((8, WIDTH), BF16),
            pltpu.VMEM((FEAT, VOCAB), BF16),
            pltpu.VMEM((1, CHIP_W), F32),
            pltpu.VMEM((2, HD, R), BF16),
            pltpu.VMEM((TOK, TOK), BF16),
            pltpu.VMEM((2, 128), jnp.int32),
            pltpu.VMEM((4, 128), jnp.int32),
            pltpu.VMEM((NS, 4, 128), jnp.int32),
            pltpu.SMEM((NS, 4, 128), jnp.int32),
            pltpu.VMEM((TOK, R), BF16),
            pltpu.VMEM((TOK, R), BF16),
            pltpu.VMEM((NX, NZ, 2, 16, WIDTH // 2), BF16),
            pltpu.VMEM((2, R, WIDTH), BF16),
            pltpu.VMEM((CHIP_W, CHIPS * HD), BF16),
            pltpu.VMEM((VOCAB // 8, 128), F32),
            pltpu.VMEM((128, 128), F32),
            pltpu.VMEM((NS, 32, 128), BF16),
            pltpu.VMEM((NS, 32, 128), BF16),
            pltpu.VMEM((TOK, HD), BF16),
            pltpu.VMEM((TOK, CHIPS * HD), BF16),
            pltpu.VMEM((TOK, TOK), BF16),
            pltpu.VMEM((TOK, CHIP_W), F32),
            pltpu.VMEM((HALF, CHIP_W), F32),
            pltpu.VMEM((TOK, WIDTH), F32),
            pltpu.VMEM((2, TOK, WIDTH), BF16),
            pltpu.VMEM((TOK, CHIP_W), BF16),
            pltpu.VMEM((TOK, 128), F32),
            pltpu.VMEM((CHIPS, TOK, HD), BF16),
            pltpu.VMEM((CHIPS, TOK, HD), BF16),
            pltpu.VMEM((8, TOK), F32),
            pltpu.VMEM((NT, 8, TOK), F32),
            pltpu.VMEM((8, HALF), F32),
            pltpu.VMEM((CHIPS, 8, HALF), F32),
            pltpu.VMEM((2, HALF, WIDTH), BF16),
            pltpu.VMEM((2, HALF, WIDTH), BF16),
            pltpu.VMEM((TOK, HD), BF16),
            pltpu.VMEM((HALF, HD), BF16),
            pltpu.VMEM((CHIPS, 2 * ROWS, R), BF16),
            pltpu.VMEM((CHIPS, 2 * ROWS, R), BF16),
            pltpu.VMEM((CHIPS, 2 * ROWS, R), BF16),
            pltpu.VMEM((CHIPS, 2 * ROWS, R), BF16),
            pltpu.VMEM((16, 128), F32),
            pltpu.VMEM((NT, 16, 128), F32),
            pltpu.SemaphoreType.DMA((28,)),
            pltpu.SemaphoreType.DMA((28,)),
            pltpu.SemaphoreType.DMA((7,)),
        ],
        compiler_params=pltpu.CompilerParams(
            collective_id=0, has_side_effects=True, vmem_limit_bytes=52 * 2**20
        ),
        name="relay",
    )(
        outgoing, returning, token_ids.reshape(2, 128), shared_basis, embed_table, norm_gain, value_weight,
        write_basis, head_logits,
    )
    return (next_out, next_ret, grad_write[None], grad_gain)


def solution(mesh):
    placed = (
        P("section", None),
        P("section", None),
        P("section"),
        P("section", None),
        P(("tensor", "section"), None),
        P("section", None),
        P("section", None, "tensor"),
        P("section", "tensor", None),
        P("section", "tensor", None, None),
    )
    return jax.shard_map(
        shards,
        mesh=mesh,
        in_specs=placed,
        out_specs=(
            P("section", None),
            P("section", None),
            P("section", "tensor", None),
            P("section", None),
        ),
        check_vma=False,
    )
```

time: 160 us -> 127 us (0.79)
  the two profiles are of different devices: /device:TPU:21 before, /device:TPU:391 now
where the time goes in v2:
time: 127 us
  Pallas kernels  118 us (93%)
  local copies, waits for them, and re-layouts  8.76 us (7%)
    pallas_call x1, Pallas kernels, shards(): pl.pallas_call(kernel, out_shape=(jax.ShapeDtypeStruct((TOK, R), BF16), j...  118 us
    unnamed x18, local copies, waits for them, and re-layouts  8.76 us

profile of v2, /device:TPU:391, one launch (start us, length us, event | category | flops | bytes accessed | tf_op | source)
XLA Modules:
  0.0 126.9 jit_solution(6022857993063174720)
XLA Ops:
  0.6 0.0 copy-start
  0.6 0.9 copy-done
  1.6 0.0 copy-start.1
  1.6 0.9 copy-done.1
  2.5 0.0 copy-start.2
  2.5 0.9 copy-done.2
  3.4 0.0 copy-start.3
  3.4 0.9 copy-done.3
  4.3 0.0 copy-start.4
  4.3 0.9 copy-done.4
  5.2 0.0 copy-start.5
  5.3 0.8 copy-done.5
  6.0 0.0 copy-start.6
  6.0 0.7 copy-done.6
  6.7 117.5 %relay.1 = (bf16[256,512]{1,0:T(8,128)(2,1)S(1)}, bf16[256,512]{1,0:T(8,128)(2,1)S(1)}, f32[128,512]{1,0:T(8,128)S(1)}, bf16[1,8192]{1,0:T(2,128)(2,1)S(1)}) custom-call(bf16[256,512]{1,0:T(8,128)(2,1)S(1)} %copy-done, bf16[256,512]{1,0:T(8,128)(2,1)S(1)} %copy-done.1, s32[2,128]{1,0:T(2,128)S(1)} %bitcast.3, bf16[8,8192]{1,0:T(8,128)(2,1)S(1)} %copy-done.2, ...), custom_call_target="tpu_custom_call" | custom-call | tf_op jit(solution)/shard_map/relay/pallas_call | solution.py:468
  124.2 0.7 copy.17
  124.9 0.7 copy.18
  125.6 0.7 copy.19
  126.3 0.6 copy.20
Async XLA Ops:
  0.6 1.0 copy-start
  1.6 0.9 copy-start.1
  2.5 0.9 copy-start.2
  3.4 0.9 copy-start.3
  4.3 0.9 copy-start.4
  5.2 0.8 copy-start.5
  6.0 0.7 copy-start.6

commit v3 on v2

--- a/solution.py
+++ b/solution.py
@@ -22,8 +22,8 @@
 CHIP_W = 2 * WIDTH
 NX = 4
 NZ = 8
-AT_Z = 12
-AT_X = 36
+SIDE = NX * NZ
+AT_X = 10
 AT_ROWS = 44
 AT_GRAD = 52
 MESH = pl.DeviceIdType.MESH
@@ -47,9 +47,9 @@
     outgoing, returning, ids, basis_hbm, table_hbm, gain_hbm, weight, write_hbm, logits_hbm,
     next_out, next_ret, grad_write, grad_gain,
     basis_own, table, gain, write, logits,
-    ids_raw, ids_own, ids_all, ids_scalar, coef, cot, pieces, basis, w_all, table_t, stage,
+    ids_raw, ids_all, ids_scalar, coef, cot, pieces, basis, w_all, table_t, stage,
     emb_out, emb_in, gv_own, gv_all, heads, gn, gn_in, res_c, res, ng, acc, v_out, v_in, st_out, st_in,
-    in_out, in_in, g_hi, g_lo, att_own, att_in, rs_out, rs_in, ag, ag_in, gg_own, gg_in,
+    in_out, in_in, g_hi, g_lo, att_own, att_in, rs_out, rs_in, rg_out, rg_in, ag, ag_in, ad, ad_in, gg_own, gg_in,
     send, recv, local,
 ):
     s = lax.axis_index("section")
@@ -57,7 +57,8 @@
     chip = t // 2
     core = lax.rem(t, 2)
     other = 1 - core
-    y_lo = s // (NX * NZ)
+    y_lo = s // SIDE
+    place = lax.rem(s, SIDE)
     z = lax.rem(s // NX, NZ)
     x = lax.rem(s, NX)
 
@@ -100,8 +101,8 @@
 
     ids_copy.wait()
     own = ids_raw[...]
-    ids_own[0:2, :] = (own >> 10) * 128 + (own & 127)
-    ids_own[2:4, :] = (own >> 7) & 7
+    ids_all[place, y_lo, 0:2, :] = (own >> 10) * 128 + (own & 127)
+    ids_all[place, y_lo, 2:4, :] = (own >> 7) & 7
     basis_copy.wait()
     part = basis_own[...].astype(F32)
     pieces[x, z, y_lo] = jnp.concatenate([part[:, : WIDTH // 2], part[:, WIDTH // 2 :]], axis=0).astype(BF16)
@@ -121,15 +122,9 @@
     here = pl.ds(pl.multiple_of(core * HALF, HALF), HALF)
     there = pl.ds(pl.multiple_of(other * HALF, HALF), HALF)
 
-    def send_ids(k, c):
-        push(ids_own, ids_all.at[s], 0, (section_peer(k), t))
-        return c
-
-    lax.fori_loop(1, NS, send_ids, 0)
-    ids_all[s] = ids_own[...]
-    push(pieces.at[x, z, y_lo], pieces.at[x, z, y_lo], 3, (lax.rem(s + NS // 2, NS), t))
-    write_copy.wait()
-    push(write.at[core], write.at[core], 18, partner)
+    facing = (lax.rem(s + SIDE, NS), t)
+    push(ids_all.at[place, y_lo], ids_all.at[place, y_lo], 19, facing)
+    push(pieces.at[x, z, y_lo], pieces.at[x, z, y_lo], 3, facing)
 
     @pl.when(s > 0)
     def _():
@@ -139,6 +134,26 @@
     def _():
         push(outgoing.at[here], coef.at[here], 1, (section_peer(1), t))
 
+
+    wait_bytes(ids_all.at[0, 0], recv.at[19])
+
+    def send_ids(k, c):
+        push(ids_all.at[place], ids_all.at[place], 0, (y_lo * SIDE + lax.rem(place + k, SIDE), t))
+        return c
+
+    lax.fori_loop(1, SIDE, send_ids, 0)
+    for k in (2, 1, 3):
+        rows = pl.ds(pl.multiple_of(chip_peer(k) * CHIP_W, CHIP_W), CHIP_W)
+        push(weight.at[0, rows], w_all.at[:, own_cols], 4, across(k))
+    wait_bytes(pieces.at[0, 0, 0], recv.at[3])
+
+    def send_z(k, c):
+        push(pieces.at[x, z], pieces.at[x, z], 11, (y_lo * SIDE + lax.rem(z + k, NZ) * NX + x, t))
+        return c
+
+    lax.fori_loop(1, NZ, send_z, 0)
+    write_copy.wait()
+    push(write.at[core], write.at[core], 18, partner)
 
     table_copy.wait()
 
@@ -149,11 +164,8 @@
         return c
 
     lax.fori_loop(0, VOCAB // 1024, turn, 0)
-    for k in (2, 1, 3):
-        rows = pl.ds(pl.multiple_of(chip_peer(k) * CHIP_W, CHIP_W), CHIP_W)
-        push(weight.at[0, rows], w_all.at[:, own_cols], 4, across(k))
-
-    wait_bytes(ids_all.at[pl.ds(0, NS - 1)], recv.at[0])
+
+    wait_bytes(ids_all.at[pl.ds(0, SIDE - 1)], recv.at[0])
     scalar_copy = fetch(ids_all, ids_scalar, 0)
     scalar_copy.wait()
     lane = lax.broadcasted_iota(jnp.int32, (8, 128), 1)
@@ -161,9 +173,11 @@
     group = lane // FEAT
 
     def find(p, half):
-        groups = jnp.broadcast_to(ids_all[p, pl.ds(2 + half, 1), :], (8, 128))
+        low = lax.rem(p, SIDE)
+        high = p // SIDE
+        groups = jnp.broadcast_to(ids_all[low, high, pl.ds(2 + half, 1), :], (8, 128))
         for j in range(128):
-            stage[pl.ds(j, 1), :] = table_t[pl.ds(ids_scalar[p, half, j], 1), :]
+            stage[pl.ds(j, 1), :] = table_t[pl.ds(ids_scalar[low, high, half, j], 1), :]
         outs = []
         for q in range(2):
             place = jnp.take_along_axis(groups, 16 * group + 8 * q + sub, axis=1) * FEAT + lane % FEAT
@@ -210,21 +224,11 @@
         lax.fori_loop(0, 2, one_half, 0)
         push(emb_out.at[p], emb_in.at[s], 6, (p, t))
 
-        @pl.when(k == AT_Z)
-        def _():
-            wait_bytes(pieces.at[0, 0, 0], recv.at[3])
-
-            def send_z(j, cc):
-                push(pieces.at[x, z], pieces.at[x, z], 11, (y_lo * NX * NZ + lax.rem(z + j, NZ) * NX + x, t))
-                return cc
-
-            lax.fori_loop(1, NZ, send_z, 0)
-
         @pl.when(k == AT_X)
         def _():
             wait_bytes(pieces.at[0, pl.ds(0, NZ - 1)], recv.at[11])
             for j in (2, 1, 3):
-                push(pieces.at[x], pieces.at[x], 12, (y_lo * NX * NZ + z * NX + lax.rem(x + j, NX), t))
+                push(pieces.at[x], pieces.at[x], 12, (y_lo * SIDE + z * NX + lax.rem(x + j, NX), t))
 
         @pl.when(jnp.logical_and(k == AT_ROWS, s < NS - 1))
         def _():
@@ -340,30 +344,47 @@
     wait_bytes(gv_all.at[:, pl.ds(0, (CHIPS - 1) * HD)], recv.at[5])
     gn[...] = dot_nt(gv_all[...], w_all[...])
     push(gn.at[there], gn_in, 15, partner)
-    wait_bytes(gn_in, recv.at[15])
-    inv = acc[here, :]
-    inner = jnp.zeros((HALF, 128), F32)
+    inner = jnp.zeros((TOK, 128), F32)
     for u in range(CHIP_W // 128):
         cols = slice(u * 128, (u + 1) * 128)
         narrow = slice(u % 8 * 128, (u % 8 + 1) * 128)
-        n = gn[here, cols] + gn_in[:, cols]
-        gn_in[:, cols] = n
-        r = res[u // 8, here, narrow].astype(F32)
-        inner = inner + n * gain[:, cols] * r
-        gg_own[u : u + 1, :] = jnp.sum(n * inv * r, axis=0, keepdims=True)
-    in_out[...] = jnp.broadcast_to(jnp.sum(inner.T, axis=0, keepdims=True), (8, HALF))
-    for k in (2, 1, 3):
-        push(in_out, in_in.at[chip], 16, across(k))
-    in_in[chip] = in_out[...]
-    wait_bytes(in_in.at[pl.ds(0, CHIPS - 1)], recv.at[16])
-    total = in_in[0]
-    for i in range(1, CHIPS):
-        total = total + in_in[i]
-    back = jnp.broadcast_to(total[0:1, :], (HALF, HALF)).T * inv * inv * inv / D
+        inner = inner + gn[:, cols] * gain[:, cols] * res[u // 8, :, narrow].astype(F32)
+    in_out[...] = jnp.broadcast_to(jnp.sum(inner.T, axis=0, keepdims=True), (8, TOK))
+
+    def send_inner(k, c):
+        push(in_out, in_in.at[t], 16, (s, tensor_peer(k)))
+        return c
+
+    lax.fori_loop(1, NT, send_inner, 0)
+    in_in[t] = in_out[...]
+
+    wait_bytes(gn_in, recv.at[15])
+    inv = acc[here, :]
     for u in range(CHIP_W // 128):
         cols = slice(u * 128, (u + 1) * 128)
         narrow = slice(u % 8 * 128, (u % 8 + 1) * 128)
-        g = gn_in[:, cols] * inv * gain[:, cols] - res[u // 8, here, narrow].astype(F32) * back
+        n = (gn[here, cols] + gn_in[:, cols]) * inv
+        gn_in[:, cols] = n * gain[:, cols]
+        gg_own[u : u + 1, :] = jnp.sum(n * res[u // 8, here, narrow].astype(F32), axis=0, keepdims=True)
+
+    wait_bytes(v_in.at[pl.ds(0, CHIPS - 1)], recv.at[7])
+    v = v_in[0].astype(F32)
+    for i in range(1, CHIPS):
+        v = v + v_in[i].astype(F32)
+    attended = dot(heads[...], v.astype(BF16))
+    att_own[...] = attended.astype(BF16)
+    push(att_own.at[there], att_in, 17, partner)
+
+    wait_bytes(in_in.at[pl.ds(0, NT - 1)], recv.at[16])
+    total = in_in[0]
+    for i in range(1, NT):
+        total = total + in_in[i]
+    acc[...] = jnp.broadcast_to(total[0:1, :], (128, TOK)).T
+    back = acc[here, :] * inv * inv * inv / D
+    for u in range(CHIP_W // 128):
+        cols = slice(u * 128, (u + 1) * 128)
+        narrow = slice(u % 8 * 128, (u % 8 + 1) * 128)
+        g = gn_in[:, cols] - res[u // 8, here, narrow].astype(F32) * back
         upper = g.astype(BF16)
         g_hi[u // 8, :, narrow] = upper
         g_lo[u // 8, :, narrow] = (g - upper.astype(F32)).astype(BF16)
@@ -372,21 +393,17 @@
     grad = grad + (dot_nt(g_hi[1], basis[1]) + dot_nt(g_lo[1], basis[1]))
     grad = grad.astype(BF16)
     for i in range(CHIPS):
-        rs_out[i, ROWS : 2 * ROWS, :] = grad[i * ROWS : (i + 1) * ROWS, :]
-
-    wait_bytes(v_in.at[pl.ds(0, CHIPS - 1)], recv.at[7])
-    v = v_in[0].astype(F32)
-    for i in range(1, CHIPS):
-        v = v + v_in[i].astype(F32)
-    attended = dot(heads[...], v.astype(BF16))
-    att_own[...] = attended.astype(BF16)
-    push(att_own.at[there], att_in, 17, partner)
+        rg_out[i] = grad[i * ROWS : (i + 1) * ROWS, :]
+    for k in (2, 1, 3):
+        push(rg_out.at[chip_peer(k)], rg_in.at[chip], 29, across(k))
+    rg_in[chip] = rg_out[chip]
+
     wait_bytes(write.at[0], recv.at[18])
     delta = dot(att_own[here, :], write[core])
     wait_bytes(att_in, recv.at[17])
     delta = (delta + dot(att_in[...], write[other])).astype(BF16)
     for i in range(CHIPS):
-        rs_out[i, 0:ROWS, :] = delta[i * ROWS : (i + 1) * ROWS, :]
+        rs_out[i] = delta[i * ROWS : (i + 1) * ROWS, :]
     for k in (2, 1, 3):
         push(rs_out.at[chip_peer(k)], rs_in.at[chip], 9, across(k))
     rs_in[chip] = rs_out[chip]
@@ -397,38 +414,47 @@
 
     lax.fori_loop(1, NT, send_gain, 0)
     gg_in[t] = gg_own[...]
+    mine = pl.ds(pl.multiple_of(core * HALF + chip * ROWS, ROWS), ROWS)
+
+    def add_up(parts, base, to_all, to_core, first):
+        total = base[mine, :].astype(F32)
+        for i in range(CHIPS):
+            total = total + parts[i].astype(F32)
+        to_all[chip] = total.astype(BF16)
+        for k in (2, 1, 3):
+            push(to_all.at[chip], to_all.at[chip], first + k, across(k))
+        push(to_all.at[chip], to_core.at[chip], first, partner)
+
+    def forward(to_all, to_core, first):
+        for k in (1, 3, 2):
+            wait_bytes(to_all.at[0], recv.at[first + k])
+            come = chip_peer(CHIPS - k)
+            push(to_all.at[come], to_core.at[come], first + 3 + k, partner)
+
+    def collect(to_all, to_core, first, out):
+        for i in range(CHIPS):
+            out[pl.ds(pl.multiple_of(core * HALF + i * ROWS, ROWS), ROWS), :] = to_all[i]
+        for which in (first, first + 4, first + 5, first + 6):
+            wait_bytes(to_core.at[0], recv.at[which])
+        for i in range(CHIPS):
+            out[pl.ds(pl.multiple_of(other * HALF + i * ROWS, ROWS), ROWS), :] = to_core[i]
+
+    wait_bytes(rg_in.at[pl.ds(0, CHIPS - 1)], recv.at[29])
+    add_up(rg_in, cot, ag, ag_in, 30)
+    wait_bytes(rs_in.at[pl.ds(0, CHIPS - 1)], recv.at[9])
+    add_up(rs_in, coef, ad, ad_in, 37)
     grad_write[...] = dot(attended.T.astype(BF16), cot[...])
-
-    wait_bytes(rs_in.at[pl.ds(0, CHIPS - 1)], recv.at[9])
-    total = rs_in[0].astype(F32)
-    for i in range(1, CHIPS):
-        total = total + rs_in[i].astype(F32)
-    mine = pl.ds(pl.multiple_of(core * HALF + chip * ROWS, ROWS), ROWS)
-    ag[chip, 0:ROWS, :] = (coef[mine, :].astype(F32) + total[0:ROWS, :]).astype(BF16)
-    ag[chip, ROWS : 2 * ROWS, :] = (cot[mine, :].astype(F32) + total[ROWS : 2 * ROWS, :]).astype(BF16)
-    for k in (2, 1, 3):
-        push(ag.at[chip], ag.at[chip], 19 + k, across(k))
-    push(ag.at[chip], ag_in.at[chip], 19, partner)
+    forward(ag, ag_in, 30)
     wait_bytes(gg_in.at[pl.ds(0, NT - 1)], recv.at[10])
     grad_gain[...] = jnp.concatenate(
         [gg_in[2 * i, j : j + 1, :] + gg_in[2 * i + 1, j : j + 1, :] for i in range(CHIPS) for j in range(16)], axis=1
     ).astype(BF16)
-    for k in (1, 3, 2):
-        wait_bytes(ag.at[0], recv.at[19 + k])
-        come = chip_peer(CHIPS - k)
-        push(ag.at[come], ag_in.at[come], 22 + k, partner)
-    for i in range(CHIPS):
-        rows = pl.ds(pl.multiple_of(core * HALF + i * ROWS, ROWS), ROWS)
-        next_out[rows, :] = ag[i, 0:ROWS, :]
-        next_ret[rows, :] = ag[i, ROWS : 2 * ROWS, :]
-    for which in (19, 23, 24, 25):
-        wait_bytes(ag_in.at[0], recv.at[which])
-    for i in range(CHIPS):
-        rows = pl.ds(pl.multiple_of(other * HALF + i * ROWS, ROWS), ROWS)
-        next_out[rows, :] = ag_in[i, 0:ROWS, :]
-        next_ret[rows, :] = ag_in[i, ROWS : 2 * ROWS, :]
-
-    wait_bytes(ids_all.at[pl.ds(0, NS - 1)], send.at[0])
+    forward(ad, ad_in, 37)
+    collect(ag, ag_in, 30, next_ret)
+    collect(ad, ad_in, 37, next_out)
+
+    wait_bytes(ids_all.at[pl.ds(0, SIDE - 1)], send.at[0])
+    wait_bytes(ids_all.at[0, 0], send.at[19])
 
     @pl.when(s < NS - 1)
     def _():
@@ -453,10 +479,11 @@
     wait_bytes(basis.at[0], send.at[13])
     wait_bytes(res.at[0], send.at[14])
     wait_bytes(gn_in, send.at[15])
-    wait_bytes(in_in.at[pl.ds(0, CHIPS - 1)], send.at[16])
+    wait_bytes(in_in.at[pl.ds(0, NT - 1)], send.at[16])
     wait_bytes(att_in, send.at[17])
     wait_bytes(write.at[0], send.at[18])
-    for which in (19, 20, 21, 22, 23, 24, 25):
+    wait_bytes(rg_in.at[pl.ds(0, CHIPS - 1)], send.at[29])
+    for which in range(30, 44):
         wait_bytes(ag_in.at[0], send.at[which])
 
 
@@ -482,9 +509,8 @@
             pltpu.VMEM((2, HD, R), BF16),
             pltpu.VMEM((TOK, TOK), BF16),
             pltpu.VMEM((2, 128), jnp.int32),
-            pltpu.VMEM((4, 128), jnp.int32),
-            pltpu.VMEM((NS, 4, 128), jnp.int32),
-            pltpu.SMEM((NS, 4, 128), jnp.int32),
+            pltpu.VMEM((SIDE, 2, 4, 128), jnp.int32),
+            pltpu.SMEM((SIDE, 2, 4, 128), jnp.int32),
             pltpu.VMEM((TOK, R), BF16),
             pltpu.VMEM((TOK, R), BF16),
             pltpu.VMEM((NX, NZ, 2, 16, WIDTH // 2), BF16),
@@ -507,20 +533,24 @@
             pltpu.VMEM((CHIPS, TOK, HD), BF16),
             pltpu.VMEM((8, TOK), F32),
             pltpu.VMEM((NT, 8, TOK), F32),
-            pltpu.VMEM((8, HALF), F32),
-            pltpu.VMEM((CHIPS, 8, HALF), F32),
+            pltpu.VMEM((8, TOK), F32),
+            pltpu.VMEM((NT, 8, TOK), F32),
             pltpu.VMEM((2, HALF, WIDTH), BF16),
             pltpu.VMEM((2, HALF, WIDTH), BF16),
             pltpu.VMEM((TOK, HD), BF16),
             pltpu.VMEM((HALF, HD), BF16),
-            pltpu.VMEM((CHIPS, 2 * ROWS, R), BF16),
-            pltpu.VMEM((CHIPS, 2 * ROWS, R), BF16),
-            pltpu.VMEM((CHIPS, 2 * ROWS, R), BF16),
-            pltpu.VMEM((CHIPS, 2 * ROWS, R), BF16),
+            pltpu.VMEM((CHIPS, ROWS, R), BF16),
+            pltpu.VMEM((CHIPS, ROWS, R), BF16),
+            pltpu.VMEM((CHIPS, ROWS, R), BF16),
+            pltpu.VMEM((CHIPS, ROWS, R), BF16),
+            pltpu.VMEM((CHIPS, ROWS, R), BF16),
+            pltpu.VMEM((CHIPS, ROWS, R), BF16),
+            pltpu.VMEM((CHIPS, ROWS, R), BF16),
+            pltpu.VMEM((CHIPS, ROWS, R), BF16),
             pltpu.VMEM((16, 128), F32),
             pltpu.VMEM((NT, 16, 128), F32),
-            pltpu.SemaphoreType.DMA((28,)),
-            pltpu.SemaphoreType.DMA((28,)),
+            pltpu.SemaphoreType.DMA((44,)),
+            pltpu.SemaphoreType.DMA((44,)),
             pltpu.SemaphoreType.DMA((7,)),
         ],
         compiler_params=pltpu.CompilerParams(

time: 127 us -> 121 us (0.953)
  the two profiles are of different devices: /device:TPU:391 before, /device:TPU:5 now
where the time goes in v3:
time: 121 us; the launch traced here: 120 us
  Pallas kernels  111 us (92%)
  local copies, waits for them, and re-layouts  8.76 us (7%)
    pallas_call x1, Pallas kernels, shards(): pl.pallas_call(kernel, out_shape=(jax.ShapeDtypeStruct((TOK, R), BF16), j...  111 us
    unnamed x18, local copies, waits for them, and re-layouts  8.76 us

profile of v3, /device:TPU:5, one launch (start us, length us, event | category | flops | bytes accessed | tf_op | source)
XLA Modules:
  0.0 120.5 jit_solution(7468726034799677480)
XLA Ops:
  0.6 0.0 copy-start
  0.6 0.9 copy-done
  1.6 0.0 copy-start.1
  1.6 0.9 copy-done.1
  2.5 0.0 copy-start.2
  2.5 0.9 copy-done.2
  3.4 0.0 copy-start.3
  3.4 0.9 copy-done.3
  4.3 0.0 copy-start.4
  4.3 0.9 copy-done.4
  5.2 0.0 copy-start.5
  5.3 0.8 copy-done.5
  6.0 0.0 copy-start.6
  6.0 0.7 copy-done.6
  6.7 111.0 %relay.1 = (bf16[256,512]{1,0:T(8,128)(2,1)S(1)}, bf16[256,512]{1,0:T(8,128)(2,1)S(1)}, f32[128,512]{1,0:T(8,128)S(1)}, bf16[1,8192]{1,0:T(2,128)(2,1)S(1)}) custom-call(bf16[256,512]{1,0:T(8,128)(2,1)S(1)} %copy-done, bf16[256,512]{1,0:T(8,128)(2,1)S(1)} %copy-done.1, s32[2,128]{1,0:T(2,128)S(1)} %bitcast.3, bf16[8,8192]{1,0:T(8,128)(2,1)S(1)} %copy-done.2, ...), custom_call_target="tpu_custom_call" | custom-call | tf_op jit(solution)/shard_map/relay/pallas_call | solution.py:495
  117.7 0.7 copy.17
  118.4 0.7 copy.18
  119.1 0.7 copy.19
  119.8 0.6 copy.20
Async XLA Ops:
  0.6 1.0 copy-start
  1.6 0.9 copy-start.1
  2.5 0.9 copy-start.2
  3.4 0.9 copy-start.3
  4.3 0.9 copy-start.4
  5.2 0.8 copy-start.5
  6.0 0.7 copy-start.6

commit v4 on v3

--- a/solution.py
+++ b/solution.py
@@ -24,6 +24,7 @@
 NZ = 8
 SIDE = NX * NZ
 AT_X = 10
+TURN_FIRST = 14
 AT_ROWS = 44
 AT_GRAD = 52
 MESH = pl.DeviceIdType.MESH
@@ -49,7 +50,7 @@
     basis_own, table, gain, write, logits,
     ids_raw, ids_all, ids_scalar, coef, cot, pieces, basis, w_all, table_t, stage,
     emb_out, emb_in, gv_own, gv_all, heads, gn, gn_in, res_c, res, ng, acc, v_out, v_in, st_out, st_in,
-    in_out, in_in, g_hi, g_lo, att_own, att_in, rs_out, rs_in, rg_out, rg_in, ag, ag_in, ad, ad_in, gg_own, gg_in,
+    in_out, in_in, g_hi, g_lo, att_own, att_in, rs_out, rs_in, rg_out, rg_in, ag, ag_in, ad, ad_in, gg_own, gg_in, gg_all, gw,
     send, recv, local,
 ):
     s = lax.axis_index("section")
@@ -135,6 +136,15 @@
         push(outgoing.at[here], coef.at[here], 1, (section_peer(1), t))
 
 
+    table_copy.wait()
+
+    def turn(b, c):
+        tile = table[:, pl.ds(pl.multiple_of(b * 1024, 1024), 1024)]
+        tile = jnp.concatenate([tile[:, v * 128 : (v + 1) * 128] for v in range(8)], axis=0)
+        table_t[pl.ds(pl.multiple_of(b * 128, 128), 128), :] = tile.T.astype(F32)
+        return c
+
+    lax.fori_loop(0, TURN_FIRST, turn, 0)
     wait_bytes(ids_all.at[0, 0], recv.at[19])
 
     def send_ids(k, c):
@@ -154,16 +164,7 @@
     lax.fori_loop(1, NZ, send_z, 0)
     write_copy.wait()
     push(write.at[core], write.at[core], 18, partner)
-
-    table_copy.wait()
-
-    def turn(b, c):
-        tile = table[:, pl.ds(pl.multiple_of(b * 1024, 1024), 1024)]
-        tile = jnp.concatenate([tile[:, v * 128 : (v + 1) * 128] for v in range(8)], axis=0)
-        table_t[pl.ds(pl.multiple_of(b * 128, 128), 128), :] = tile.astype(F32).T
-        return c
-
-    lax.fori_loop(0, VOCAB // 1024, turn, 0)
+    lax.fori_loop(TURN_FIRST, VOCAB // 1024, turn, 0)
 
     wait_bytes(ids_all.at[pl.ds(0, SIDE - 1)], recv.at[0])
     scalar_copy = fetch(ids_all, ids_scalar, 0)
@@ -176,8 +177,10 @@
         low = lax.rem(p, SIDE)
         high = p // SIDE
         groups = jnp.broadcast_to(ids_all[low, high, pl.ds(2 + half, 1), :], (8, 128))
-        for j in range(128):
-            stage[pl.ds(j, 1), :] = table_t[pl.ds(ids_scalar[low, high, half, j], 1), :]
+        for j in range(0, 128, 16):
+            found = [table_t[pl.ds(ids_scalar[low, high, half, j + i], 1), :] for i in range(16)]
+            for i in range(16):
+                stage[pl.ds(j + i, 1), :] = found[i]
         outs = []
         for q in range(2):
             place = jnp.take_along_axis(groups, 16 * group + 8 * q + sub, axis=1) * FEAT + lane % FEAT
@@ -187,6 +190,7 @@
                 found = row if found is None else jnp.where(group == b, row, found)
             outs.append(found)
         return jnp.concatenate(outs, axis=0).astype(BF16)
+
 
     def values_gradient():
         logits_copy.wait()
@@ -333,14 +337,6 @@
 
     w_copy.wait()
     wait_bytes(w_all.at[:, pl.ds(0, (CHIPS - 1) * HD)], recv.at[4])
-    for h in range(2):
-        v = dot(ng[...], w_all[:, h * 256 : (h + 1) * 256]).astype(BF16)
-        v_out[2 * h] = v[:, :HD]
-        v_out[2 * h + 1] = v[:, HD:]
-    for k in (2, 1, 3):
-        push(v_out.at[chip_peer(k)], v_in.at[chip], 7, across(k))
-    v_in[chip] = v_out[chip]
-
     wait_bytes(gv_all.at[:, pl.ds(0, (CHIPS - 1) * HD)], recv.at[5])
     gn[...] = dot_nt(gv_all[...], w_all[...])
     push(gn.at[there], gn_in, 15, partner)
@@ -357,6 +353,14 @@
 
     lax.fori_loop(1, NT, send_inner, 0)
     in_in[t] = in_out[...]
+
+    for h in range(2):
+        v = dot(ng[...], w_all[:, h * 256 : (h + 1) * 256]).astype(BF16)
+        v_out[2 * h] = v[:, :HD]
+        v_out[2 * h + 1] = v[:, HD:]
+    for k in (2, 1, 3):
+        push(v_out.at[chip_peer(k)], v_in.at[chip], 7, across(k))
+    v_in[chip] = v_out[chip]
 
     wait_bytes(gn_in, recv.at[15])
     inv = acc[here, :]
@@ -431,27 +435,36 @@
             come = chip_peer(CHIPS - k)
             push(to_all.at[come], to_core.at[come], first + 3 + k, partner)
 
-    def collect(to_all, to_core, first, out):
+    def put(parts, whose, out, which):
         for i in range(CHIPS):
-            out[pl.ds(pl.multiple_of(core * HALF + i * ROWS, ROWS), ROWS), :] = to_all[i]
-        for which in (first, first + 4, first + 5, first + 6):
-            wait_bytes(to_core.at[0], recv.at[which])
-        for i in range(CHIPS):
-            out[pl.ds(pl.multiple_of(other * HALF + i * ROWS, ROWS), ROWS), :] = to_core[i]
+            rows = pl.ds(pl.multiple_of(whose * HALF + i * ROWS, ROWS), ROWS)
+            pltpu.make_async_copy(parts.at[i], out.at[rows], local.at[which]).start()
+
+    def collect(to_all, to_core, first, out, which):
+        put(to_all, core, out, which)
+        for k in (first, first + 4, first + 5, first + 6):
+            wait_bytes(to_core.at[0], recv.at[k])
+        put(to_core, other, out, which)
 
     wait_bytes(rg_in.at[pl.ds(0, CHIPS - 1)], recv.at[29])
     add_up(rg_in, cot, ag, ag_in, 30)
     wait_bytes(rs_in.at[pl.ds(0, CHIPS - 1)], recv.at[9])
     add_up(rs_in, coef, ad, ad_in, 37)
-    grad_write[...] = dot(attended.T.astype(BF16), cot[...])
+    gw[...] = dot(attended.T.astype(BF16), cot[...])
+    gw_copy = fetch(gw, grad_write, 3)
     forward(ag, ag_in, 30)
     wait_bytes(gg_in.at[pl.ds(0, NT - 1)], recv.at[10])
-    grad_gain[...] = jnp.concatenate(
+    gg_all[...] = jnp.concatenate(
         [gg_in[2 * i, j : j + 1, :] + gg_in[2 * i + 1, j : j + 1, :] for i in range(CHIPS) for j in range(16)], axis=1
     ).astype(BF16)
+    gg_copy = fetch(gg_all, grad_gain, 4)
     forward(ad, ad_in, 37)
-    collect(ag, ag_in, 30, next_ret)
-    collect(ad, ad_in, 37, next_out)
+    collect(ag, ag_in, 30, next_ret, 1)
+    collect(ad, ad_in, 37, next_out, 2)
+    wait_bytes(next_ret, local.at[1])
+    wait_bytes(next_out, local.at[2])
+    gw_copy.wait()
+    gg_copy.wait()
 
     wait_bytes(ids_all.at[pl.ds(0, SIDE - 1)], send.at[0])
     wait_bytes(ids_all.at[0, 0], send.at[19])
@@ -487,21 +500,34 @@
         wait_bytes(ag_in.at[0], send.at[which])
 
 
+def hand_over(a, b, c, d, a_out, b_out, c_out, d_out, a_here, b_here, c_here, d_here, sem):
+    steps = ((a, a_here, a_out), (b, b_here, b_out), (c, c_here, c_out), (d, d_here, d_out))
+    into = [pltpu.make_async_copy(src, here, sem.at[i]) for i, (src, here, _) in enumerate(steps)]
+    out = [pltpu.make_async_copy(here, dst, sem.at[4 + i]) for i, (_, here, dst) in enumerate(steps)]
+    for copy in into:
+        copy.start()
+    for first, second in zip(into, out):
+        first.wait()
+        second.start()
+    for copy in out:
+        copy.wait()
+
+
 def shards(
     outgoing, returning, token_ids, shared_basis, embed_table, norm_gain, value_weight, write_basis, head_logits
 ):
-    vmem = pl.BlockSpec(memory_space=pltpu.VMEM)
     hbm = pl.BlockSpec(memory_space=pl.ANY)
-    next_out, next_ret, grad_write, grad_gain = pl.pallas_call(
+    results = (
+        jax.ShapeDtypeStruct((TOK, R), BF16),
+        jax.ShapeDtypeStruct((TOK, R), BF16),
+        jax.ShapeDtypeStruct((HD, R), F32),
+        jax.ShapeDtypeStruct((1, D), BF16),
+    )
+    made = pl.pallas_call(
         kernel,
-        out_shape=(
-            jax.ShapeDtypeStruct((TOK, R), BF16),
-            jax.ShapeDtypeStruct((TOK, R), BF16),
-            jax.ShapeDtypeStruct((HD, R), F32),
-            jax.ShapeDtypeStruct((1, D), BF16),
-        ),
+        out_shape=results,
         in_specs=[hbm] * 9,
-        out_specs=(vmem, vmem, vmem, vmem),
+        out_specs=(hbm,) * 4,
         scratch_shapes=[
             pltpu.VMEM((8, WIDTH), BF16),
             pltpu.VMEM((FEAT, VOCAB), BF16),
@@ -549,18 +575,35 @@
             pltpu.VMEM((CHIPS, ROWS, R), BF16),
             pltpu.VMEM((16, 128), F32),
             pltpu.VMEM((NT, 16, 128), F32),
+            pltpu.VMEM((1, D), BF16),
+            pltpu.VMEM((HD, R), F32),
             pltpu.SemaphoreType.DMA((44,)),
             pltpu.SemaphoreType.DMA((44,)),
             pltpu.SemaphoreType.DMA((7,)),
         ],
         compiler_params=pltpu.CompilerParams(
-            collective_id=0, has_side_effects=True, vmem_limit_bytes=52 * 2**20
+            collective_id=0, has_side_effects=True, vmem_limit_bytes=63 * 2**20
         ),
         name="relay",
     )(
         outgoing, returning, token_ids.reshape(2, 128), shared_basis, embed_table, norm_gain, value_weight,
         write_basis, head_logits,
     )
+    next_out, next_ret, grad_write, grad_gain = pl.pallas_call(
+        hand_over,
+        out_shape=results,
+        in_specs=[hbm] * 4,
+        out_specs=(hbm,) * 4,
+        scratch_shapes=[
+            pltpu.VMEM((TOK, R), BF16),
+            pltpu.VMEM((TOK, R), BF16),
+            pltpu.VMEM((HD, R), F32),
+            pltpu.VMEM((1, D), BF16),
+            pltpu.SemaphoreType.DMA((8,)),
+        ],
+        compiler_params=pltpu.CompilerParams(vmem_limit_bytes=63 * 2**20),
+        name="hand_over",
+    )(*made)
     return (next_out, next_ret, grad_write[None], grad_gain)
 
 

time: 121 us -> 114 us (0.942)
  the two profiles are of different devices: /device:TPU:5 before, /device:TPU:9 now
where the time goes in v4:
time: 114 us
  Pallas kernels  113 us (99%)
    pallas_call x1, Pallas kernels, shards(): pl.pallas_call(kernel, out_shape=results, in_specs=[hbm] * 9, out_specs=(...  112 us

profile of v4, /device:TPU:9, one launch (start us, length us, event | category | flops | bytes accessed | tf_op | source)
XLA Modules:
  0.0 114.1 jit_solution(7939841587367384261)
XLA Ops:
  0.6 111.6 %relay.1 = (bf16[256,512]{1,0:T(8,128)(2,1)}, bf16[256,512]{1,0:T(8,128)(2,1)}, f32[128,512]{1,0:T(8,128)}, bf16[1,8192]{1,0:T(2,128)(2,1)}) custom-call(bf16[256,512]{1,0:T(8,128)(2,1)} %outgoing.1, bf16[256,512]{1,0:T(8,128)(2,1)} %returning.1, s32[2,128]{1,0:T(2,128)} %bitcast.2, bf16[8,8192]{1,0:T(8,128)(2,1)} %basis_hbm.1, bf16[16,65536]{1,0:T(8,128)(2,1)} %table_hbm.1, ...), custom_call_target="tpu_custom_call" | custom-call | tf_op jit(solution)/shard_map/relay/pallas_call | solution.py:526
  112.2 1.9 %hand_over.1 = (bf16[256,512]{1,0:T(8,128)(2,1)}, bf16[256,512]{1,0:T(8,128)(2,1)}, f32[128,512]{1,0:T(8,128)}, bf16[1,8192]{1,0:T(2,128)(2,1)}) custom-call(bf16[256,512]{1,0:T(8,128)(2,1)} %get-tuple-element.12.a, bf16[256,512]{1,0:T(8,128)(2,1)} %get-tuple-element.13.b, f32[128,512]{1,0:T(8,128)} %get-tuple-element.14.c, bf16[1,8192]{1,0:T(2,128)(2,1)} %get-tuple-element.15.d), custom_call_target="tpu_custom_call" | custom-call | tf_op jit(solution)/shard_map/hand_over/pallas_call | solution.py:592

commit v5 on v4

--- a/solution.py
+++ b/solution.py
@@ -453,12 +453,12 @@
     gw[...] = dot(attended.T.astype(BF16), cot[...])
     gw_copy = fetch(gw, grad_write, 3)
     forward(ag, ag_in, 30)
+    forward(ad, ad_in, 37)
     wait_bytes(gg_in.at[pl.ds(0, NT - 1)], recv.at[10])
     gg_all[...] = jnp.concatenate(
         [gg_in[2 * i, j : j + 1, :] + gg_in[2 * i + 1, j : j + 1, :] for i in range(CHIPS) for j in range(16)], axis=1
     ).astype(BF16)
     gg_copy = fetch(gg_all, grad_gain, 4)
-    forward(ad, ad_in, 37)
     collect(ag, ag_in, 30, next_ret, 1)
     collect(ad, ad_in, 37, next_out, 2)
     wait_bytes(next_ret, local.at[1])

time: 114 us -> 114 us (level)
  no operation moved by 1% of the time
where the time goes in v5:
time: 114 us
  Pallas kernels  113 us (99%)
    pallas_call x1, Pallas kernels, shards(): pl.pallas_call(kernel, out_shape=results, in_specs=[hbm] * 9, out_specs=(...  112 us

profile of v5, /device:TPU:9, one launch (start us, length us, event | category | flops | bytes accessed | tf_op | source)
XLA Modules:
  0.0 114.1 jit_solution(11130703323013280515)
XLA Ops:
  0.6 111.6 %relay.1 = (bf16[256,512]{1,0:T(8,128)(2,1)}, bf16[256,512]{1,0:T(8,128)(2,1)}, f32[128,512]{1,0:T(8,128)}, bf16[1,8192]{1,0:T(2,128)(2,1)}) custom-call(bf16[256,512]{1,0:T(8,128)(2,1)} %outgoing.1, bf16[256,512]{1,0:T(8,128)(2,1)} %returning.1, s32[2,128]{1,0:T(2,128)} %bitcast.2, bf16[8,8192]{1,0:T(8,128)(2,1)} %basis_hbm.1, bf16[16,65536]{1,0:T(8,128)(2,1)} %table_hbm.1, ...), custom_call_target="tpu_custom_call" | custom-call | tf_op jit(solution)/shard_map/relay/pallas_call | solution.py:526
  112.2 1.9 %hand_over.1 = (bf16[256,512]{1,0:T(8,128)(2,1)}, bf16[256,512]{1,0:T(8,128)(2,1)}, f32[128,512]{1,0:T(8,128)}, bf16[1,8192]{1,0:T(2,128)(2,1)}) custom-call(bf16[256,512]{1,0:T(8,128)(2,1)} %get-tuple-element.12.a, bf16[256,512]{1,0:T(8,128)(2,1)} %get-tuple-element.13.b, f32[128,512]{1,0:T(8,128)} %get-tuple-element.14.c, bf16[1,8192]{1,0:T(2,128)(2,1)} %get-tuple-element.15.d), custom_call_target="tpu_custom_call" | custom-call | tf_op jit(solution)/shard_map/hand_over/pallas_call | solution.py:592
